TPU v7x, 128 devices: a whole 4x4x4 slice. The times are simulated.
128 devices in a mesh: row: 8 (over z, x_hi), col: 16 (over y, x_lo, core).
Axes of the slice: x: 4 (x_hi: 2, x_lo: 2; x = x_hi * 2 + x_lo), y: 4, z: 4, core: 2. Of those that a mesh axis runs over, the one named last changes fastest.
Arguments:
- tokens: bfloat16 [16384, 1024], P(('row', 'col')), may hold values from -6 to 6
- cotangent: bfloat16 [16384, 1024], P(('row', 'col')), may hold values from -6 to 6
- deal_order: int32 [8, 2048], P('row'), may hold values from 0 to 2047, as said below
- lengths: int32 [8, 4], P('row'), may hold values from 1 to 1024, 2048 in all within a row
- routes: int32 [16384, 8], P(('row', 'col')), may hold values from 0 to 31, all different within a row; in each aligned block of 128 rows (0 to 127, 128 to 255, ...) at most 64 rows name the same one
- route_gates: float32 [16384, 8], P(('row', 'col')), may hold values from 0.25 to 0.75
- gain_first: float32 [1024], replicated, may hold values from 0.1 to 1.9
- gain_second: float32 [1024], replicated, may hold values from 0.1 to 1.9
- gain_query: float32 [64], replicated, may hold values from 0.1 to 1.9
- gain_key: float32 [64], replicated, may hold values from 0.1 to 1.9
- weight_qkv: float32 [1024, 2048], P('row', 'col'), may hold values from -0.1875 to 0.1875
- weight_out: float32 [1024, 1024], P('row', 'col'), may hold values from -1.5 to 1.5
- weight_gate: float32 [1024, 32, 512], P('row', 'col'), may hold values from -0.1875 to 0.1875
- weight_up: float32 [1024, 32, 512], P('row', 'col'), may hold values from -0.1875 to 0.1875
- weight_down: float32 [1024, 32, 512], P('row', 'col'), may hold values from -0.25 to 0.25
Outputs:
- block_out: bfloat16 [16384, 1024], P(('row', 'col'))
- input_grad: bfloat16 [16384, 1024], P(('row', 'col'))
- grad_first: float32 [1024], replicated
- grad_second: float32 [1024], replicated
- grad_query: float32 [64], replicated
- grad_key: float32 [64], replicated
- grad_qkv: float32 [1024, 2048], P('row', 'col')
- grad_out: float32 [1024, 1024], P('row', 'col')
- grad_gate: float32 [1024, 32, 512], P('row', 'col')
- grad_up: float32 [1024, 32, 512], P('row', 'col')
- grad_down: float32 [1024, 32, 512], P('row', 'col')
Inputs may be any that keep to these rules, and one draw needn't show every extreme that they name: `deal_order`: each row is a permutation of 0 to 2047. With the slots and the given rows of a group cut into 16 blocks of 128, every block of slots takes exactly 8 rows of every block of given rows. `routes`: within the rows of one device no expert is named more than 64 times; some device names some expert exactly 64 times. `lengths`: each row sums to 2048.
All inputs are finite; a program needn't handle non-finite values.
Results may differ from a plain program's by a relative error of at most 0.025.
Values may be sent and summed in bfloat16 or wider, within the bound.
No kernel may reach another device: no remote copies, remote signals or barrier semaphores. Data moves between devices by JAX's collectives and lax.ppermute only.
A program may use at most 128 MiB of HBM per device.

v0:
```python
from functools import partial

import jax
import jax.numpy as jnp
from jax import lax
from jax.sharding import PartitionSpec as P

HEADS = 16
KV_HEADS = 8
HEAD_DIM = 64
EXPERTS = 32
TOP = 8
TOK_DEV = 128
CAP = 64


EPS_WIDE = 1e-05
EPS_HEAD = 1e-06
THETA = 10000.0
MASKED = -1e30


def swapped(block, axis, distance):
    count = lax.axis_size(axis)
    route = []
    for low in range(count):
        high = low | 1 << distance
        if high != low and high < count:
            route += [(low, high), (high, low)]
    return lax.ppermute(block, axis, route)


def norm_rows(values, scales, epsilon):
    factor = lax.rsqrt(jnp.mean(values * values, axis=-1, keepdims=True) + epsilon)
    return values * factor * scales


def rotary(values, cosine_table, sine_table):
    middle = values.shape[-1] // 2
    leading = values[..., :middle]
    trailing = values[..., middle:]
    return jnp.concatenate(
        [
            leading * cosine_table - trailing * sine_table,
            trailing * cosine_table + leading * sine_table,
        ],
        axis=-1,
    )


def tables(lengths_row, amount, head_width):
    finish = jnp.cumsum(lengths_row)
    starts = finish - lengths_row
    positions = jnp.arange(amount, dtype=jnp.int32)
    segment = jnp.sum((positions[:, None] >= finish[None, :]).astype(jnp.int32), axis=1)
    labels = jnp.arange(lengths_row.shape[0], dtype=jnp.int32)
    anchor = jnp.sum(jnp.where(segment[:, None] == labels[None, :], starts[None, :], 0), axis=1)
    offset = (positions - anchor).astype(jnp.float32)
    frequency = THETA ** (-jnp.arange(head_width // 2, dtype=jnp.float32) * 2.0 / head_width)
    angles = offset[:, None] * frequency[None, :]
    return (segment, jnp.cos(angles), jnp.sin(angles))


def attend_forward(query_head, keys_all, values_all, segment, block_rows, scaling):
    amount = query_head.shape[0]
    blocks = amount // block_rows

    def one_block(block_index):
        anchor = block_index * block_rows
        block_query = lax.dynamic_slice_in_dim(query_head, anchor, block_rows, 0)
        labels = lax.dynamic_slice_in_dim(segment, anchor, block_rows, 0)
        scores = (
            jnp.einsum("qd,kd->qk", block_query, keys_all, preferred_element_type=jnp.float32)
            * scaling
        )
        scores = jnp.where(labels[:, None] == segment[None, :], scores, MASKED)
        highest = jnp.max(scores, axis=1, keepdims=True)
        weights = jnp.exp(scores - highest)
        totals = jnp.sum(weights, axis=1, keepdims=True)
        probs = (weights / totals).astype(jnp.bfloat16)
        result = jnp.dot(probs, values_all, preferred_element_type=jnp.float32).astype(jnp.bfloat16)
        return (result, (highest + jnp.log(totals))[:, 0])

    results, logsum = lax.map(one_block, jnp.arange(blocks, dtype=jnp.int32))
    return (results.reshape(amount, -1), logsum.reshape(amount))


def attend_backward(
    query_head, keys_all, values_all, segment, logsum, grad_head, block_rows, scaling
):
    amount = query_head.shape[0]
    blocks = amount // block_rows

    def one_block(running, block_index):
        key_sum, value_sum = running
        anchor = block_index * block_rows
        block_query = lax.dynamic_slice_in_dim(query_head, anchor, block_rows, 0)
        labels = lax.dynamic_slice_in_dim(segment, anchor, block_rows, 0)
        block_lse = lax.dynamic_slice_in_dim(logsum, anchor, block_rows, 0)
        block_grad = lax.dynamic_slice_in_dim(grad_head, anchor, block_rows, 0)
        scores = (
            jnp.einsum("qd,kd->qk", block_query, keys_all, preferred_element_type=jnp.float32)
            * scaling
        )
        scores = jnp.where(labels[:, None] == segment[None, :], scores, MASKED)
        probs = jnp.exp(scores - block_lse[:, None])
        prob_grad = jnp.einsum(
            "qd,kd->qk", block_grad, values_all, preferred_element_type=jnp.float32
        )
        centre = jnp.sum(probs * prob_grad, axis=1, keepdims=True)
        score_grad = (probs * (prob_grad - centre)).astype(jnp.bfloat16)
        query_grad = jnp.dot(score_grad, keys_all, preferred_element_type=jnp.float32) * scaling
        key_sum = (
            key_sum
            + jnp.einsum("qk,qd->kd", score_grad, block_query, preferred_element_type=jnp.float32)
            * scaling
        )
        value_sum = value_sum + jnp.einsum(
            "qk,qd->kd", probs.astype(jnp.bfloat16), block_grad, preferred_element_type=jnp.float32
        )
        return ((key_sum, value_sum), query_grad)

    empty_state = (jnp.zeros(keys_all.shape, jnp.float32), jnp.zeros(values_all.shape, jnp.float32))
    (key_sum, value_sum), query_grad = lax.scan(
        one_block, empty_state, jnp.arange(blocks, dtype=jnp.int32)
    )
    return (query_grad.reshape(amount, -1), key_sum, value_sum)


def collect(local_rows):
    return lax.all_gather(local_rows, "col", axis=0, tiled=True)


def body(
    tokens,
    cotangent,
    deal_order,
    lengths,
    routes,
    route_gates,
    gain_first,
    gain_second,
    gain_query,
    gain_key,
    weight_qkv,
    weight_out,
    weight_gate,
    weight_up,
    weight_down,
):
    peers = lax.axis_size("col")
    column = lax.axis_index("col")
    group_tok = TOK_DEV * peers
    share = TOK_DEV // peers
    split = peers // KV_HEADS
    heads_here = HEADS // peers
    slots_here = 4 // split
    member = column % split
    first_head = member * heads_here
    experts_here = EXPERTS // peers
    block_rows = min(512, group_tok)
    width = tokens.shape[1]
    scaling = HEAD_DIM ** (-0.5)
    deal_row = deal_order[0]
    counting = jnp.arange(TOK_DEV, dtype=jnp.int32)
    inverse = (
        jnp.zeros((group_tok,), jnp.int32).at[deal_row].set(jnp.arange(group_tok, dtype=jnp.int32))
    )
    own_slots = column * TOK_DEV + counting
    leave = jnp.argsort(inverse[own_slots])
    sent_rows, sent_grad = (
        lax.all_to_all(
            tokens[leave].reshape(peers, share, width),
            "col",
            split_axis=0,
            concat_axis=0,
            tiled=True,
        ),
        lax.all_to_all(
            cotangent[leave].reshape(peers, share, width),
            "col",
            split_axis=0,
            concat_axis=0,
            tiled=True,
        ),
    )
    arrive_key = deal_row[own_slots] // TOK_DEV * group_tok + own_slots
    arrival = jnp.zeros((TOK_DEV,), jnp.int32).at[jnp.argsort(arrive_key)].set(counting)
    dealt = sent_rows.reshape(TOK_DEV, width)[arrival].astype(jnp.float32)
    upstream = sent_grad.reshape(TOK_DEV, width)[arrival].astype(jnp.float32)
    full_qkv, full_out, full_gate, full_up, full_down = (
        lax.all_gather(weight_qkv.astype(jnp.bfloat16), "row", axis=0, tiled=True),
        lax.all_gather(weight_out.astype(jnp.bfloat16), "row", axis=0, tiled=True),
        lax.all_gather(weight_gate.astype(jnp.bfloat16), "row", axis=0, tiled=True),
        lax.all_gather(weight_up.astype(jnp.bfloat16), "row", axis=0, tiled=True),
        lax.all_gather(weight_down.astype(jnp.bfloat16), "row", axis=0, tiled=True),
    )
    normed, first_pull = jax.vjp(partial(norm_rows, epsilon=EPS_WIDE), dealt, gain_first)
    normed_low = normed.astype(jnp.bfloat16)
    gathered = collect(normed_low)
    segment, cosine_table, sine_table = tables(lengths[0], group_tok, HEAD_DIM)
    raw = jnp.dot(gathered, full_qkv, preferred_element_type=jnp.float32)
    roles = member * slots_here + jnp.arange(slots_here, dtype=jnp.int32)

    def shape_heads(block, scale_query, scale_key):
        split_heads = block.reshape(group_tok, slots_here, HEAD_DIM)
        scales = jnp.where((roles < 2)[:, None], scale_query[None, :], scale_key[None, :])
        turned = rotary(
            norm_rows(split_heads, scales, EPS_HEAD),
            cosine_table[:, None, :],
            sine_table[:, None, :],
        )
        chosen = jnp.where((roles == 3)[None, :, None], split_heads, turned)
        return chosen.reshape(group_tok, slots_here * HEAD_DIM)

    shaped, shape_pull = jax.vjp(shape_heads, raw, gain_query, gain_key)
    own_low = shaped.astype(jnp.bfloat16)
    partner = swapped(own_low, "col", 0)
    whole = jnp.where(
        member == 0,
        jnp.concatenate([own_low, partner], axis=1),
        jnp.concatenate([partner, own_low], axis=1),
    )
    heads_all = whole.reshape(group_tok, 4, HEAD_DIM)
    queries = lax.dynamic_slice_in_dim(heads_all, first_head, heads_here, 1)
    keys_all = heads_all[:, 2]
    values_all = heads_all[:, 3]
    head_index = 0
    result_head, logsum_head = attend_forward(
        queries[:, head_index], keys_all, values_all, segment, block_rows, scaling
    )
    logsums = [logsum_head]
    portion = result_head
    attention_rows = lax.psum_scatter(
        lax.dot_general(
            portion, full_out, (((1,), (1,)), ((), ())), preferred_element_type=jnp.float32
        ).astype(jnp.bfloat16),
        "col",
        scatter_dimension=0,
        tiled=True,
    ).astype(jnp.float32)
    hidden = dealt + attention_rows
    middle, second_pull = jax.vjp(partial(norm_rows, epsilon=EPS_WIDE), hidden, gain_second)
    middle_low = middle.astype(jnp.bfloat16)
    flat_routes = routes.reshape(-1)
    expert_ids = jnp.arange(EXPERTS, dtype=jnp.int32)
    onehot = (flat_routes[:, None] == expert_ids[None, :]).astype(jnp.int32)
    ranks = jnp.sum(jnp.cumsum(onehot, axis=0) * onehot, axis=1) - 1
    slot_index = flat_routes * CAP + ranks
    route_count = flat_routes.shape[0]
    owner = (
        jnp.full((EXPERTS * CAP,), -1, jnp.int32)
        .at[slot_index]
        .set(jnp.arange(route_count, dtype=jnp.int32))
    )
    filled = owner >= 0
    route_of = jnp.maximum(owner, 0)
    token_of = route_of // TOP
    flat_gates = route_gates.reshape(-1)
    zero_rows = jnp.zeros((EXPERTS * CAP, width), jnp.bfloat16)
    send_rows = jnp.where(filled[:, None], middle_low[token_of], zero_rows).reshape(
        peers, experts_here, CAP, width
    )
    scaled_grad = (flat_gates[route_of][:, None] * upstream[token_of]).astype(jnp.bfloat16)
    send_grad = jnp.where(filled[:, None], scaled_grad, zero_rows).reshape(
        peers, experts_here, CAP, width
    )
    expert_rows, expert_grad = (
        lax.all_to_all(send_rows, "col", split_axis=0, concat_axis=0, tiled=True),
        lax.all_to_all(send_grad, "col", split_axis=0, concat_axis=0, tiled=True),
    )
    gate_pre = jnp.einsum(
        "nemd,def->nemf", expert_rows, full_gate, preferred_element_type=jnp.float32
    )
    up_pre = jnp.einsum("nemd,def->nemf", expert_rows, full_up, preferred_element_type=jnp.float32)
    gate_sigmoid = jax.nn.sigmoid(gate_pre)
    activated = gate_pre * gate_sigmoid
    inner = (activated * up_pre).astype(jnp.bfloat16)
    result = jnp.einsum(
        "nemf,def->nemd", inner, full_down, preferred_element_type=jnp.float32
    ).astype(jnp.bfloat16)
    inner_grad = jnp.einsum(
        "nemd,def->nemf", expert_grad, full_down, preferred_element_type=jnp.float32
    )
    gate_grad = (
        inner_grad * up_pre * gate_sigmoid * (1.0 + gate_pre * (1.0 - gate_sigmoid))
    ).astype(jnp.bfloat16)
    up_grad = (inner_grad * activated).astype(jnp.bfloat16)
    down_total = jnp.einsum(
        "nemf,nemd->def", inner, expert_grad, preferred_element_type=jnp.float32
    )
    gate_total = jnp.einsum(
        "nemd,nemf->def", expert_rows, gate_grad, preferred_element_type=jnp.float32
    )
    up_total = jnp.einsum(
        "nemd,nemf->def", expert_rows, up_grad, preferred_element_type=jnp.float32
    )
    entry_grad = (
        jnp.einsum("nemf,def->nemd", gate_grad, full_gate, preferred_element_type=jnp.float32)
        + jnp.einsum("nemf,def->nemd", up_grad, full_up, preferred_element_type=jnp.float32)
    ).astype(jnp.bfloat16)
    returned_rows, returned_grad = (
        lax.all_to_all(result, "col", split_axis=0, concat_axis=0, tiled=True),
        lax.all_to_all(entry_grad, "col", split_axis=0, concat_axis=0, tiled=True),
    )
    picked_rows = (
        returned_rows.reshape(EXPERTS * CAP, width)[slot_index]
        .reshape(TOK_DEV, TOP, width)
        .astype(jnp.float32)
    )
    expert_sum = jnp.sum(picked_rows * route_gates[:, :, None], axis=1)
    picked_grad = (
        returned_grad.reshape(EXPERTS * CAP, width)[slot_index]
        .reshape(TOK_DEV, TOP, width)
        .astype(jnp.float32)
    )
    middle_grad = jnp.sum(picked_grad, axis=1)
    output_rows = (hidden + expert_sum).astype(jnp.bfloat16)
    hidden_back, second_gain = second_pull(middle_grad)
    hidden_grad = upstream + hidden_back
    hidden_low = hidden_grad.astype(jnp.bfloat16)
    portion = lax.all_gather(hidden_low, "col", axis=0, tiled=True)
    local_grad = jnp.dot(portion, full_out, preferred_element_type=jnp.float32)
    weight_sum = lax.dot_general(
        portion, result_head, (((0,), (0,)), ((), ())), preferred_element_type=jnp.float32
    )
    joined_low = local_grad.astype(jnp.bfloat16)
    head_index = 0
    query_part, key_part, value_part = attend_backward(
        queries[:, head_index],
        keys_all,
        values_all,
        segment,
        logsums[head_index],
        joined_low,
        block_rows,
        scaling,
    )
    query_grads = [query_part]
    full_grad = jnp.zeros((group_tok, 4, HEAD_DIM), jnp.float32)
    full_grad = lax.dynamic_update_slice_in_dim(
        full_grad, jnp.stack(query_grads, axis=1), first_head, 1
    )
    full_grad = full_grad.at[:, 2].set(key_part).at[:, 3].set(value_part)
    kept_half = lax.dynamic_slice_in_dim(full_grad, member * 2, 2, 1)
    other_half = lax.dynamic_slice_in_dim(full_grad, (1 - member) * 2, 2, 1)
    block_grad = kept_half + swapped(other_half.astype(jnp.bfloat16), "col", 0).astype(
        other_half.dtype
    )
    raw_grad, query_gain, key_gain = shape_pull(
        block_grad.reshape(group_tok, slots_here * HEAD_DIM)
    )
    raw_low = raw_grad.astype(jnp.bfloat16)
    again = collect(normed_low)
    qkv_total = lax.dot_general(
        again, raw_low, (((0,), (0,)), ((), ())), preferred_element_type=jnp.float32
    )
    portion = raw_low
    normed_grad = lax.psum_scatter(
        lax.dot_general(
            portion, full_qkv, (((1,), (1,)), ((), ())), preferred_element_type=jnp.float32
        ).astype(jnp.bfloat16),
        "col",
        scatter_dimension=0,
        tiled=True,
    ).astype(jnp.float32)
    dealt_back, first_gain = first_pull(normed_grad)
    input_low = (hidden_grad + dealt_back).astype(jnp.bfloat16)
    depart = jnp.argsort(deal_row[own_slots])
    back_rows, back_grad = (
        lax.all_to_all(
            output_rows[depart].reshape(peers, share, width),
            "col",
            split_axis=0,
            concat_axis=0,
            tiled=True,
        ),
        lax.all_to_all(
            input_low[depart].reshape(peers, share, width),
            "col",
            split_axis=0,
            concat_axis=0,
            tiled=True,
        ),
    )
    home_key = inverse[own_slots] // TOK_DEV * group_tok + own_slots
    homing = jnp.zeros((TOK_DEV,), jnp.int32).at[jnp.argsort(home_key)].set(counting)
    block_out = back_rows.reshape(TOK_DEV, width)[homing]
    input_grad = back_grad.reshape(TOK_DEV, width)[homing]
    grad_qkv, grad_out, grad_gate, grad_up, grad_down = (
        lax.psum_scatter(
            qkv_total.astype(jnp.bfloat16), "row", scatter_dimension=0, tiled=True
        ).astype(jnp.float32),
        lax.psum_scatter(
            weight_sum.astype(jnp.bfloat16), "row", scatter_dimension=0, tiled=True
        ).astype(jnp.float32),
        lax.psum_scatter(
            gate_total.astype(jnp.bfloat16), "row", scatter_dimension=0, tiled=True
        ).astype(jnp.float32),
        lax.psum_scatter(
            up_total.astype(jnp.bfloat16), "row", scatter_dimension=0, tiled=True
        ).astype(jnp.float32),
        lax.psum_scatter(
            down_total.astype(jnp.bfloat16), "row", scatter_dimension=0, tiled=True
        ).astype(jnp.float32),
    )
    grad_first, grad_second, grad_query, grad_key = lax.psum(
        (first_gain, second_gain, query_gain, key_gain), ("row", "col")
    )
    return (
        block_out,
        input_grad,
        grad_first,
        grad_second,
        grad_query,
        grad_key,
        grad_qkv,
        grad_out,
        grad_gate,
        grad_up,
        grad_down,
    )


def solution(mesh):
    return jax.shard_map(
        body,
        mesh=mesh,
        in_specs=(
            P(("row", "col"), None),
            P(("row", "col"), None),
            P("row", None),
            P("row", None),
            P(("row", "col"), None),
            P(("row", "col"), None),
            P(),
            P(),
            P(),
            P(),
            P("row", "col"),
            P("row", "col"),
            P("row", "col", None),
            P("row", "col", None),
            P("row", "col", None),
        ),
        out_specs=(
            P(("row", "col"), None),
            P(("row", "col"), None),
            P(),
            P(),
            P(),
            P(),
            P("row", "col"),
            P("row", "col"),
            P("row", "col", None),
            P("row", "col", None),
            P("row", "col", None),
        ),
        check_vma=False,
    )
```

profile of v0, /device:TPU:1, one launch (start us, length us, event | category | flops | bytes accessed | tf_op | source)
XLA Modules:
  0.0 1110.8 jit_solution(14311996311694940239)
XLA Ops:
  8.9 8.0 scatter_custom_fusion
  22.3 6.9 all-to-all-start
  40.6 30.7 %all_gather.23 = bf16[1024,128]{1,0:T(8,128)(2,1)S(1)} all-gather(bf16[128,128]{1,0:T(8,128)(2,1)S(1)} %convert_element_type.172), channel_id=1, replica_groups=mesh['row'=8,'col'=16] {'row'}, dimensions={0}, use_global_device_ids=true | all-gather | bytes 294912 | tf_op jit(solution)/shard_map/all_gather | solution.py:192
  72.4 8.5 all-gather.6.cloned.1.call-done
  80.9 3.7 multiply_reduce_fusion.3
  86.2 26.1 %all_gather.24 = bf16[1024,64]{0,1:T(8,128)(2,1)S(1)} all-gather(bf16[128,64]{0,1:T(8,128)(2,1)S(1)} %convert_element_type.175), channel_id=1, replica_groups=mesh['row'=8,'col'=16] {'row'}, dimensions={0}, use_global_device_ids=true | all-gather | bytes 147456 | tf_op jit(solution)/shard_map/all_gather | solution.py:193
  114.3 21.3 %while.29 = (s32[]{:T(128)}, bf16[4,512,64]{1,2,0:T(8,128)(2,1)S(1)}, f32[4,512]{1,0:T(4,128)}, s32[4]{0:T(128)S(1)}, s32[2048]{0:T(1024)S(1)}, /*index=5*/bf16[...) while((s32[]{:T(128)}, ...), condition=%wide.region_12.13_spmd, body=%wide.region_9.12_spmd.sunk | while | flops 277904896 | bytes 13863111 | solution.py:84
  142.7 8.9 all-to-all-start.4
  152.1 9.0 reduce-window.11
  161.7 4.3 scatter_custom_fusion.2
  166.4 8.6 gather_fusion.10
  176.0 9.9 gather_fusion.11
  185.9 39.1 %reduce-scatter.14.cloned.1.call-done = bf16[128,1024]{1,0:T(8,128)(2,1)} async-done(((bf16[2048,1024]{1,0:T(8,128)(2,1)}), bf16[128,1024]{1,0:T(8,128)(2,1)}) %reduce-scatter.14.cloned.1.call-update) | async-done | bytes 262160 | tf_op jit(solution)/shard_map/reduce_scatter | solution.py:234
  227.7 9.7 gather_fusion.4
  237.3 7.9 fusion.19
  245.2 7.5 all-to-all-start.1
  253.6 60.8 %all-to-all-done.1 = bf16[16,2,64,1024]{3,2,1,0:T(8,128)(2,1)} async-done(((bf16[16,2,64,1024]{3,2,1,0:T(8,128)(2,1)}), bf16[16,2,64,1024]{3,2,1,0:T(8,128)(2,1)}, u32[]{:S(2)}, u32[]{:S(2)}) %all-to-all-start.1) | async-done | bytes 4194336 | tf_op jit(solution)/shard_map/all_to_all | solution.py:269
  314.4 6.2 all-to-all-start.5
  321.9 7.2 fusion.37
  329.1 7.1 fusion.39
  336.2 55.3 %all-gather.12.cloned.1.call-done = bf16[1024,2,512]{2,0,1:T(8,128)(2,1)} async-done(((bf16[128,2,512]{2,0,1:T(8,128)(2,1)}), bf16[1024,2,512]{2,0,1:T(8,128)(2,1)}) %all-gather.12.cloned.1.call-update) | async-done | bytes 2097168 | tf_op jit(solution)/shard_map/all_gather | solution.py:196
  391.6 10.6 fusion.25
  410.2 5.3 all-to-all-start.6
  415.7 49.5 %all-to-all-done.6 = bf16[16,2,64,1024]{3,2,1,0:T(8,128)(2,1)} async-done(((bf16[16,2,64,1024]{3,2,1,0:T(8,128)(2,1)}), bf16[16,2,64,1024]{3,2,1,0:T(8,128)(2,1)}, u32[]{:S(2)}, u32[]{:S(2)}) %all-to-all-start.6) | async-done | bytes 4194336 | tf_op jit(solution)/shard_map/all_to_all | solution.py:304
  465.2 7.7 gather_fusion.12
  479.8 34.2 %all-gather.14.cloned.1.call-done = bf16[2048,1024]{1,0:T(8,128)(2,1)} async-done(((bf16[128,1024]{1,0:T(8,128)(2,1)}), bf16[2048,1024]{1,0:T(8,128)(2,1)}) %all-gather.14.cloned.1.call-update) | async-done | bytes 4194320 | tf_op jit(solution)/shard_map/all_gather | solution.py:322
  514.0 3.6 convolution_convert_fusion.2
  517.6 39.3 %while.30 = (s32[]{:T(128)}, f32[2048,64]{0,1:T(8,128)S(1)}, f32[2048,64]{0,1:T(8,128)S(1)}, f32[4,512,64]{1,0,2:T(4,128)}, s32[4]{0:T(128)S(1)}, /*index=5*/s32...) while((s32[]{:T(128)}, f32[2048,64]{0,1:T(8,128)S(1)}, ...), condition=%wide.region_27.28_spmd.clone, body=%wide.region_25.27_spmd.clone.sunk | while | flops 682262016 | bytes 35938548 | solution.py:124
  523.8 3.6 dynamic_update_slice.24
  533.6 3.6 dynamic_update_slice.24
  543.4 3.6 dynamic_update_slice.24
  553.2 3.6 dynamic_update_slice.24
  568.9 5.2 bitcast_convert_fusion.2
  576.8 5.3 bitcast_convert_fusion.1
  584.7 4.6 convert_bitcast_fusion
  591.8 4.7 all-to-all-start.2
  596.6 6.0 fusion.53
  605.4 67.7 %all-to-all-done.2 = bf16[16,2,64,1024]{3,2,1,0:T(8,128)(2,1)} async-done(((bf16[16,2,64,1024]{3,2,1,0:T(8,128)(2,1)}), bf16[16,2,64,1024]{3,2,1,0:T(8,128)(2,1)}, u32[]{:S(2)}, u32[]{:S(2)}) %all-to-all-start.2) | async-done | bytes 4194336 | tf_op jit(solution)/shard_map/all_to_all | solution.py:303
  673.1 7.8 gather_fusion.5
  691.3 4.1 all-to-all-start.7
  695.5 4.2 convolution_convert_fusion.3
  703.9 4.3 all-to-all-start.3
  708.2 24.7 %reduce-scatter.24.cloned.1.call-done = bf16[128,1024]{1,0:T(8,128)(2,1)} async-done(((bf16[1024,1024]{1,0:T(8,128)(2,1)}), bf16[128,1024]{1,0:T(8,128)(2,1)}) %reduce-scatter.24.cloned.1.call-update) | async-done | bytes 262160
  734.9 75.4 %reduce-scatter.26.cloned.1.call-done = bf16[128,1024]{1,0:T(8,128)(2,1)} async-done(((bf16[1024,1024]{1,0:T(8,128)(2,1)}), bf16[128,1024]{1,0:T(8,128)(2,1)}) %reduce-scatter.26.cloned.1.call-update) | async-done | bytes 262160
  812.4 75.6 %reduce-scatter.20.cloned.1.call-done = bf16[128,2,512]{2,0,1:T(8,128)(2,1)} async-done(((bf16[1024,2,512]{2,0,1:T(8,128)(2,1)}), bf16[128,2,512]{2,0,1:T(8,128)(2,1)}) %reduce-scatter.20.cloned.1.call-update) | async-done | bytes 262160 | tf_op jit(solution)/shard_map/reduce_scatter | solution.py:403
  890.1 69.7 %reduce-scatter.22.cloned.1.call-done = bf16[128,64]{1,0:T(8,128)(2,1)} async-done(((bf16[1024,64]{1,0:T(8,128)(2,1)}), bf16[128,64]{1,0:T(8,128)(2,1)}) %reduce-scatter.22.cloned.1.call-update) | async-done | bytes 16400
  961.4 70.9 %reduce-scatter.18.cloned.1.call-done = bf16[128,128]{1,0:T(8,128)(2,1)} async-done(((bf16[1024,128]{1,0:T(8,128)(2,1)}), bf16[128,128]{1,0:T(8,128)(2,1)}) %reduce-scatter.18.cloned.1.call-update) | async-done | bytes 32784 | tf_op jit(solution)/shard_map/reduce_scatter | solution.py:391
  1033.6 66.3 %all-reduce.2 = (f32[1024]{0:T(1024)}, f32[1024]{0:T(1024)}, f32[64]{0:T(128)}, f32[64]{0:T(128)}) all-reduce(f32[1024]{0:T(1024)S(1)} %get-tuple-element.278, f32[1024]{0:T(1024)S(1)} %copy-done.42, f32[64]{0:T(128)S(1)} %get-tuple-element.281, f32[64]{0:T(128)S(1)} %get-tuple-element.280), channel_id=1, replica_groups=mesh['row'=8,'col'=16] {'row','col'}, use_global_device_ids=true, to_apply=%region_32.33 | all-reduce | flops 2176 | bytes 17408 | tf_op jit(solution)/shard_map/psum | solution.py:407
  (380 shorter events, 140.7 us)
Async XLA Ops:
  8.0 12.7 %copy-start = (bf16[128,1024]{1,0:T(8,128)(2,1)S(1)}, bf16[128,1024]{1,0:T(8,128)(2,1)}, u32[]{:S(2)}) copy-start(bf16[128,1024]{1,0:T(8,128)(2,1)} %param.23) | copy-start | bytes 786436
  8.0 31.0 %copy-start.39 = (f32[1024]{0:T(1024)S(1)}, f32[1024]{0:T(1024)}, u32[]{:S(2)}) copy-start(f32[1024]{0:T(1024)} %param.29) | copy-start | bytes 12292
  8.0 32.0 %copy-start.66 = (s32[1,4]{1,0:T(1,128)S(1)}, s32[1,4]{1,0:T(1,128)}, u32[]{:S(2)}) copy-start(s32[1,4]{1,0:T(1,128)} %param.26) | copy-start | bytes 52
  8.1 32.3 %copy-start.38 = (f32[128,128]{1,0:T(8,128)S(1)}, f32[128,128]{1,0:T(8,128)}, u32[]{:S(2)}) copy-start(f32[128,128]{1,0:T(8,128)} %param.33) | copy-start | bytes 196612
  8.1 63.2 %copy-start.62 = (f32[64]{0:T(128)S(1)}, f32[64]{0:T(128)}, u32[]{:S(2)}) copy-start(f32[64]{0:T(128)} %param.32) | copy-start | bytes 772
  8.1 63.2 %copy-start.63 = (f32[64]{0:T(128)S(1)}, f32[64]{0:T(128)}, u32[]{:S(2)}) copy-start(f32[64]{0:T(128)} %param.31) | copy-start | bytes 772
  22.3 15.8 %all-to-all-start = ((bf16[16,8,1024]{2,1,0:T(8,128)(2,1)}), bf16[16,8,1024]{2,1,0:T(8,128)(2,1)S(1)}, u32[]{:S(2)}, u32[]{:S(2)}) async-start(bf16[16,8,1024]{2,1,0:T(8,128)(2,1)} %bitcast.6), calls=%async_computation | async-start | bytes 524288 | tf_op jit(solution)/shard_map/all_to_all | solution.py:172
  29.2 51.7 %all-gather.6.cloned.1.call-start = ((), (), s32[]{:S(2)}) async-start(), calls=%async_computation.15 | async-start | bytes 4456448 | tf_op jit(solution)/shard_map/all_gather | solution.py:131
  39.1 32.3 %copy-start.50 = (f32[128]{0:T(128)}, f32[128]{0:T(128)S(1)}, u32[]{:S(2)}) copy-start(f32[128]{0:T(128)S(1)} %fusion.87) | copy-start | bytes 1540
  39.9 185.0 %reduce-scatter.14.cloned.1.call-start = ((), (), s32[]{:S(2)}) async-start(), calls=%async_computation.16 | async-start | bytes 4456448 | tf_op jit(solution)/shard_map/reduce_scatter | solution.py:234
  40.2 31.1 %copy-start.55 = (pred[2]{0:T(512)(128)(4,1)}, pred[2]{0:T(512)(128)(4,1)S(1)}, u32[]{:S(2)}) copy-start(pred[2]{0:T(512)(128)(4,1)S(1)} %get-tuple-element.350) | copy-start | bytes 10
  40.2 31.1 %copy-start.57 = (pred[2]{0:T(512)(128)(4,1)}, pred[2]{0:T(512)(128)(4,1)S(1)}, u32[]{:S(2)}) copy-start(pred[2]{0:T(512)(128)(4,1)S(1)} %get-tuple-element.351) | copy-start | bytes 10
  71.3 14.2 %copy-start.21 = (bf16[1024,128]{1,0:T(8,128)(2,1)}, bf16[1024,128]{1,0:T(8,128)(2,1)S(1)}, u32[]{:S(2)}) copy-start(bf16[1024,128]{1,0:T(8,128)(2,1)S(1)} %all_gather.23) | copy-start | bytes 786436
  71.4 14.1 %copy-start.46 = (f32[2,64]{1,0:T(2,128)}, f32[2,64]{1,0:T(2,128)S(1)}, u32[]{:S(2)}) copy-start(f32[2,64]{1,0:T(2,128)S(1)} %broadcast_select_fusion.1) | copy-start | bytes 1540
  72.4 13.1 %copy-start.17 = (f32[2048,32]{0,1:T(8,128)}, f32[2048,32]{0,1:T(8,128)S(1)}, u32[]{:S(2)}) copy-start(f32[2048,32]{0,1:T(8,128)S(1)} %get-tuple-element.340) | copy-start | bytes 786436
  72.4 13.1 %copy-start.19 = (f32[2048,32]{0,1:T(8,128)}, f32[2048,32]{0,1:T(8,128)S(1)}, u32[]{:S(2)}) copy-start(f32[2048,32]{0,1:T(8,128)S(1)} %get-tuple-element.341) | copy-start | bytes 786436
  84.6 27.6 %copy-start.35 = (f32[2048,2]{0,1:T(2,128)}, f32[2048,2]{0,1:T(2,128)S(1)}, u32[]{:S(2)}) copy-start(f32[2048,2]{0,1:T(2,128)S(1)} %get-tuple-element.346) | copy-start | bytes 49156
  85.8 26.9 %collective-permute-start = (bf16[2048,128]{0,1:T(8,128)(2,1)S(1)}, bf16[2048,128]{0,1:T(8,128)(2,1)S(1)}, u32[]{:S(2)}, u32[]{:S(2)}) collective-permute-start(bf16[2048,128]{0,1:T(8,128)(2,1)S(1)} %fusion.57), channel_id=1, source_target_pairs={{0,1},{1,0},{2,3},{3,2},{4,5},{5,4},{6,7},{7,6},{8,9},{9,8},{10,11... | collective-permute-start | bytes 1572872 | tf_op jit(solution)/shard_map/ppermute | solution.py:30
  140.2 11.4 %copy-start.43 = (s32[128,8]{0,1:T(8,128)S(1)}, s32[128,8]{0,1:T(8,128)}, u32[]{:S(2)}) copy-start(s32[128,8]{0,1:T(8,128)} %param.27) | copy-start | bytes 12292
  140.2 25.8 %copy-start.52 = (f32[128,8]{0,1:T(8,128)S(1)}, f32[128,8]{0,1:T(8,128)}, u32[]{:S(2)}) copy-start(f32[128,8]{0,1:T(8,128)} %param.28) | copy-start | bytes 12292
  140.3 181.6 %all-gather.10.cloned.1.call-start = ((), (), s32[]{:S(2)}) async-start(), calls=%async_computation.18 | async-start | bytes 2359296 | tf_op jit(solution)/shard_map/all_gather | solution.py:195
  142.7 32.3 %all-to-all-start.4 = ((bf16[16,8,1024]{2,1,0:T(8,128)(2,1)}), bf16[16,8,1024]{2,1,0:T(8,128)(2,1)S(1)}, u32[]{:S(2)}, u32[]{:S(2)}) async-start(bf16[16,8,1024]{2,1,0:T(8,128)(2,1)} %bitcast.38), calls=%async_computation.5 | async-start | bytes 524288 | tf_op jit(solution)/shard_map/all_to_all | solution.py:179
  166.2 8.8 copy-start.28
  175.9 9.9 copy-start.14
  176.0 50.6 %copy-start.37 = (f32[1024]{0:T(1024)S(1)}, f32[1024]{0:T(1024)}, u32[]{:S(2)}) copy-start(f32[1024]{0:T(1024)} %param.30) | copy-start | bytes 12292
  226.6 10.8 copy-start.48
  245.2 69.1 %all-to-all-start.1 = ((bf16[16,2,64,1024]{3,2,1,0:T(8,128)(2,1)}), bf16[16,2,64,1024]{3,2,1,0:T(8,128)(2,1)}, u32[]{:S(2)}, u32[]{:S(2)}) async-start(bf16[16,2,64,1024]{3,2,1,0:T(8,128)(2,1)} %get-tuple-element.343), calls=%async_computation.2 | async-start | bytes 8388608 | tf_op jit(solution)/shard_map/all_to_all | solution.py:269
  252.7 76.3 %all-gather.8.cloned.1.call-start = ((), (), s32[]{:S(2)}) async-start(), calls=%async_computation.17 | async-start | bytes 2359296 | tf_op jit(solution)/shard_map/all_gather | solution.py:194
  314.4 77.2 %all-to-all-start.5 = ((bf16[16,2,64,1024]{3,2,1,0:T(8,128)(2,1)}), bf16[16,2,64,1024]{3,2,1,0:T(8,128)(2,1)}, u32[]{:S(2)}, u32[]{:S(2)}) async-start(bf16[16,2,64,1024]{3,2,1,0:T(8,128)(2,1)} %get-tuple-element.342), calls=%async_computation.6 | async-start | bytes 8388608 | tf_op jit(solution)/shard_map/all_to_all | solution.py:270
  320.6 71.0 %all-gather.12.cloned.1.call-start = ((), (), s32[]{:S(2)}) async-start(), calls=%async_computation.19 | async-start | bytes 2359296 | tf_op jit(solution)/shard_map/all_gather | solution.py:196
  336.2 66.0 %copy-start.24 = (bf16[1024,2,512]{2,0,1:T(8,128)(2,1)S(1)}, bf16[1024,2,512]{2,0,1:T(8,128)(2,1)}, u32[]{:S(2)}) copy-start(bf16[1024,2,512]{2,0,1:T(8,128)(2,1)} %all-gather.8.cloned.1.call-done) | copy-start | bytes 6291460
  410.2 55.1 %all-to-all-start.6 = ((bf16[16,2,64,1024]{3,2,1,0:T(8,128)(2,1)}), bf16[16,2,64,1024]{3,2,1,0:T(8,128)(2,1)}, u32[]{:S(2)}, u32[]{:S(2)}) async-start(bf16[16,2,64,1024]{3,2,1,0:T(8,128)(2,1)} %copy.111), calls=%async_computation.7 | async-start | bytes 8388608 | tf_op jit(solution)/shard_map/all_to_all | solution.py:304
  415.5 98.5 %all-gather.14.cloned.1.call-start = ((), (), s32[]{:S(2)}) async-start(), calls=%async_computation.20 | async-start | bytes 4456448 | tf_op jit(solution)/shard_map/all_gather | solution.py:322
  474.3 43.2 %copy-start.11 = (bf16[2048,64]{1,0:T(8,128)(2,1)S(1)}, bf16[2048,64]{1,0:T(8,128)(2,1)}, u32[]{:S(2)}) copy-start(bf16[2048,64]{1,0:T(8,128)(2,1)} %copy-done.10) | copy-start | bytes 786436
  479.0 208.2 %reduce-scatter.16.cloned.1.call-start = ((), (), s32[]{:S(2)}) async-start(), calls=%async_computation.21 | async-start | bytes 4456448 | tf_op jit(solution)/shard_map/reduce_scatter | solution.py:359
  560.1 2.0 collective-permute-start.1
  568.7 164.2 %reduce-scatter.24.cloned.1.call-start = ((), (), s32[]{:S(2)}) async-start(), calls=%async_computation.25 | async-start | bytes 2359296
  576.8 233.6 %reduce-scatter.26.cloned.1.call-start = ((), (), s32[]{:S(2)}) async-start(), calls=%async_computation.26 | async-start | bytes 2359296
  591.8 81.3 %all-to-all-start.2 = ((bf16[16,2,64,1024]{3,2,1,0:T(8,128)(2,1)}), bf16[16,2,64,1024]{3,2,1,0:T(8,128)(2,1)}, u32[]{:S(2)}, u32[]{:S(2)}) async-start(bf16[16,2,64,1024]{3,2,1,0:T(8,128)(2,1)} %copy.107), calls=%async_computation.3 | async-start | bytes 8388608 | tf_op jit(solution)/shard_map/all_to_all | solution.py:303
  596.5 291.5 %reduce-scatter.20.cloned.1.call-start = ((), (), s32[]{:S(2)}) async-start(), calls=%async_computation.23 | async-start | bytes 2359296 | tf_op jit(solution)/shard_map/reduce_scatter | solution.py:403
  602.5 357.3 %reduce-scatter.22.cloned.1.call-start = ((), (), s32[]{:S(2)}) async-start(), calls=%async_computation.24 | async-start | bytes 294912
  686.2 9.3 copy-start.13
  691.3 12.6 %all-to-all-start.7 = ((bf16[16,8,1024]{2,1,0:T(8,128)(2,1)}), bf16[16,8,1024]{2,1,0:T(8,128)(2,1)S(1)}, u32[]{:S(2)}, u32[]{:S(2)}) async-start(bf16[16,8,1024]{2,1,0:T(8,128)(2,1)} %bitcast.51), calls=%async_computation.9 | async-start | bytes 524288 | tf_op jit(solution)/shard_map/all_to_all | solution.py:378
  695.4 336.8 %reduce-scatter.18.cloned.1.call-start = ((), (), s32[]{:S(2)}) async-start(), calls=%async_computation.22 | async-start | bytes 294912 | tf_op jit(solution)/shard_map/reduce_scatter | solution.py:391
  699.7 261.6 %copy-start.56 = (pred[2]{0:T(512)(128)(4,1)S(1)}, pred[2]{0:T(512)(128)(4,1)}, u32[]{:S(2)}) copy-start(pred[2]{0:T(512)(128)(4,1)} %copy-done.55) | copy-start | bytes 10
  699.7 333.9 %copy-start.42 = (f32[1024]{0:T(1024)S(1)}, f32[1024]{0:T(1024)}, u32[]{:S(2)}) copy-start(f32[1024]{0:T(1024)} %get-tuple-element.276) | copy-start | bytes 12292
  703.9 397.6 %all-to-all-start.3 = ((bf16[16,8,1024]{2,1,0:T(8,128)(2,1)}), bf16[16,8,1024]{2,1,0:T(8,128)(2,1)S(1)}, u32[]{:S(2)}, u32[]{:S(2)}) async-start(bf16[16,8,1024]{2,1,0:T(8,128)(2,1)} %bitcast.36), calls=%async_computation.4 | async-start | bytes 524288 | tf_op jit(solution)/shard_map/all_to_all | solution.py:371
  708.2 394.9 %copy-start.1 = (bf16[128,1024]{1,0:T(8,128)(2,1)S(1)}, bf16[128,1024]{1,0:T(8,128)(2,1)}, u32[]{:S(2)}) copy-start(bf16[128,1024]{1,0:T(8,128)(2,1)} %param.23) | copy-start | bytes 786436
  (42 other events, 176.0 us)
Sparse Core Ops, SparseCore 0:
  40.1 40.7 all-gather.5
  140.4 84.5 reduce-scatter.13
  479.1 34.8 all-gather.13
  568.8 83.6 reduce-scatter.15
  656.0 76.7 reduce-scatter.23
  736.4 73.8 reduce-scatter.25
  814.1 73.9 reduce-scatter.19
  891.6 68.1 reduce-scatter.21
  963.3 68.8 reduce-scatter.17
Sparse Core Ops, SparseCore 1:
  143.6 57.1 all-gather.9
  256.1 67.7 all-gather.7
  326.6 64.9 all-gather.11
where the time goes:
time: 1120 us; the launch traced here: 1110 us
  waiting for transfers between devices  635 us (57%)
  local copies, waits for them, and re-layouts  129 us (12%)
  blocking collectives  123 us (11%)
  matrix products  96.3 us (9%)
  other arithmetic  54.5 us (5%)
  starting transfers between devices  50.2 us (4%)
  between operations  17.3 us (2%)
    unnamed x15, waiting for transfers between devices  170 us
    reduce_scatter x1, waiting for transfers between devices, body(): lax.psum_scatter(down_total.astype(jnp.bfloat16), 'row', scatter_dimensio...  75.6 us
    reduce_scatter x1, waiting for transfers between devices, body(): lax.psum_scatter(qkv_total.astype(jnp.bfloat16), 'row', scatter_dimension...  70.9 us
    all_to_all x1, waiting for transfers between devices, body(): lax.all_to_all(result, 'col', split_axis=0, concat_axis=0, tiled=True)  67.7 us
    psum x1, blocking collectives, body(): lax.psum((first_gain, second_gain, query_gain, key_gain), ('row', 'col'))  66.3 us
    all_to_all x1, waiting for transfers between devices, body(): lax.all_to_all(send_rows, 'col', split_axis=0, concat_axis=0, tiled=True)  60.8 us
    all_gather x1, waiting for transfers between devices, body(): lax.all_gather(weight_down.astype(jnp.bfloat16), 'row', axis=0, tiled=True)  55.3 us
    all_to_all x1, waiting for transfers between devices, body(): lax.all_to_all(entry_grad, 'col', split_axis=0, concat_axis=0, tiled=True)  49.5 us
  transfers between devices with their start and end apart: 22, of which 14 were waited for; matrix products, arithmetic and copies ran while one was open for 13% of the time, Pallas kernels for 0%

commit v1 on v0

v1 whole, which is shorter than its diff:
```python
from functools import partial

import jax
import jax.numpy as jnp
import numpy as np
from jax import lax
from jax.experimental import pallas as pl
from jax.experimental.pallas import tpu as pltpu
from jax.sharding import PartitionSpec as P

D = 1024
HEAD = 64
EXPERTS = 32
FF = 512
TOP = 8
TOK = 128
GROUP = 2048
PLANE = 1024
EPS_WIDE = 1e-05
EPS_HEAD = 1e-06
THETA = 10000.0
LOG2E = 1.4426950408889634
LN2 = 0.6931471805599453
QSCALE = LOG2E * HEAD**-0.5
APART = -256.0
BF = jnp.bfloat16
F32 = jnp.float32
NT = (((1,), (1,)), ((), ()))
TN = (((0,), (0,)), ((), ()))
HIGH = lax.Precision.HIGHEST


def params(mib=48):
    return pltpu.CompilerParams(vmem_limit_bytes=mib * 2**20)


def dot(a, b, dims=None):
    if dims is None:
        dims = (((1,), (0,)), ((), ()))
    return lax.dot_general(a, b, dims, preferred_element_type=F32)


def sds(shape, kind):
    return jax.ShapeDtypeStruct(shape, kind)


def whole(*shape):
    return pl.BlockSpec(shape, lambda *_: (0,) * len(shape))


def together(*values):
    return lax.optimization_barrier(values)


AHEAD = (1, 3, 2)


def step_pair(v, axis):
    if axis == "row":
        route = [(i, i ^ 1) for i in range(8)]
    else:
        route = [(i, i ^ 2) for i in range(16)]
    return lax.ppermute(v, axis, route)


def step_ring(v, axis, d):
    if axis == "row":
        route = [(i, (i + 2 * d) % 8) for i in range(8)]
    else:
        route = [(i, (i + 4 * d) % 16) for i in range(16)]
    return lax.ppermute(v, axis, route)


def step_core(v):
    return lax.ppermute(v, "col", [(i, i ^ 1) for i in range(16)])


def place(axis):
    i = lax.axis_index(axis)
    if axis == "col":
        i = i // 2
    return i // 2, i % 2


def gather_first(v, axis):
    h = v.shape[0] // 2
    va, vb = v[:h], v[h:]
    ax = step_pair(va, axis)
    by = [step_ring(vb, axis, d) for d in AHEAD]
    ax, *by = together(ax, *by)
    pa = jnp.stack([ax, va])
    pb = jnp.stack(by + [vb])
    return pa, pb


def gather_second(pa, pb, axis):
    bx = step_pair(pb, axis)
    ay = [step_ring(pa, axis, d) for d in AHEAD]
    return ay + [pa], [bx, pb]


def gather_plain(v, axis):
    pair = jnp.stack([step_pair(v, axis), v])
    return [step_ring(pair, axis, d) for d in AHEAD] + [pair]


def scatter_pieces(send_a, keep_a, send_b, axis):
    ra = step_pair(send_a, axis)
    rb = [step_ring(send_b[i], axis, d) for i, d in enumerate(AHEAD)]
    ra, *rb = together(ra, *rb)
    kind = send_a.dtype
    qa = [(keep_a[i].astype(F32) + ra[i].astype(F32)).astype(kind) for i in range(4)]

    def total(i):
        t = send_b[3][i].astype(F32)
        for r in rb:
            t = t + r[i].astype(F32)
        return t.astype(kind)

    qb = [total(0), total(1)]
    sa = [step_ring(qa[i], axis, d) for i, d in enumerate(AHEAD)]
    sb = step_pair(qb[0], axis)
    return sa + [qa[3]], [sb, qb[1]]


def added(terms):
    t = terms[0].astype(F32)
    for r in terms[1:]:
        t = t + r.astype(F32)
    return t


def sum_all(v):
    for k in (0, 1, 2, 3):
        v = v + lax.ppermute(v, "col", [(i, i ^ (1 << k)) for i in range(16)])
    for k in (0, 1, 2):
        v = v + lax.ppermute(v, "row", [(i, i ^ (1 << k)) for i in range(8)])
    return v


def head_sums():
    i = np.arange(256) // HEAD
    return jnp.asarray((i[:, None] == i[None, :]) / HEAD, BF)


def spread():
    s = np.zeros((256, 512), np.float32)
    for h in range(4):
        for i in range(64):
            s[h * 64 + i, h * 128 + i] = 1.0
    return jnp.asarray(s, BF)


def exact_sums(v, sums):
    hi = v.astype(BF)
    lo = (v - hi.astype(F32)).astype(BF)
    return dot(hi, sums) + dot(lo, sums)


def half_turn(v, lane):
    back = jnp.concatenate([pltpu.roll(v[:, :128], 96, 1), pltpu.roll(v[:, 128:], 96, 1)], 1)
    ahead = jnp.concatenate([pltpu.roll(v[:, :128], 32, 1), pltpu.roll(v[:, 128:], 32, 1)], 1)
    return jnp.where(lane % 64 < 32, -back, ahead)


def wide_tables(c, s, lane):
    c = jnp.where(lane < 192, jnp.concatenate([c, c], 1), 1.0)
    s = jnp.where(lane < 192, jnp.concatenate([s, s], 1), 0.0)
    return c, s


def heads_kernel(x_ref, w_ref, g_ref, c_ref, s_ref, seg_ref, bd_ref, sp_ref,
                 q0_ref, q1_ref, k_ref, v_ref, raw_ref, f_ref):
    x = x_ref[...]
    xf = x.astype(F32)
    f = lax.rsqrt(jnp.mean(xf * xf, axis=1, keepdims=True) + EPS_WIDE)
    raw = dot(x, w_ref[...]) * f
    raw_ref[...] = raw
    f_ref[...] = f
    rows = raw.shape[0]
    lane = lax.broadcasted_iota(jnp.int32, (rows, 256), 1)
    fac = jnp.where(lane < 192, lax.rsqrt(exact_sums(raw * raw, bd_ref[...]) + EPS_HEAD), 1.0)
    h = raw * fac * g_ref[...]
    c, s = wide_tables(c_ref[...], s_ref[...], lane)
    t = h * c + half_turn(h, lane) * s
    t = jnp.where(lane < 128, t * QSCALE, t).astype(BF)
    wide = dot(t, sp_ref[...])
    l1 = lax.broadcasted_iota(jnp.int32, (rows, 128), 1)
    seg = seg_ref[...]
    inseg = (l1 >= 64) & (l1 < 68)
    same = (l1 - 64) == seg
    aug_q = jnp.where(inseg & jnp.logical_not(same), APART, 0.0)
    aug_k = jnp.where((inseg & same) | ((l1 >= 68) & (l1 < 71)), 1.0, 0.0)
    aug_v = jnp.where((l1 >= 64) & (l1 < 67), 1.0, 0.0)
    q0_ref[...] = (wide[:, 0:128] + aug_q).astype(BF)
    q1_ref[...] = (wide[:, 128:256] + aug_q).astype(BF)
    k_ref[...] = (wide[:, 256:384] + aug_k).astype(BF)
    v_ref[...] = (wide[:, 384:512] + aug_v).astype(BF)


def project_heads(x, w, gains, cos, sin, seg):
    t = 512
    rows = lambda m: pl.BlockSpec((t, m), lambda i: (i, 0))
    return pl.pallas_call(
        heads_kernel,
        grid=(GROUP // t,),
        in_specs=[rows(D), whole(D, 256), whole(1, 256), rows(128), rows(128), rows(1),
                  whole(256, 256), whole(256, 512)],
        out_specs=[rows(128)] * 4 + [rows(256), rows(1)],
        out_shape=[sds((GROUP, 128), BF)] * 4 + [sds((GROUP, 256), F32), sds((GROUP, 1), F32)],
        compiler_params=params(),
        name="project_heads",
    )(x, w, gains, cos, sin, seg, head_sums(), spread())


CHUNK = 512


def attend_kernel(s_ref, q0_ref, q1_ref, k_ref, v_ref, o_ref, l_ref):
    q = jnp.concatenate([q0_ref[...], q1_ref[...]], 0)
    acc = jnp.zeros((256, 128), F32)
    for j in range(GROUP // CHUNK):
        rows = pl.ds(j * CHUNK, CHUNK)
        s = dot(q, k_ref[rows, :], NT)
        p = jnp.exp2(s).astype(BF)
        acc = acc + dot(p, v_ref[rows, :])
    total = acc[:, 64:65]
    o = acc / total
    l_ref[0] = jnp.log2(total)
    lane = lax.broadcasted_iota(jnp.int32, (128, 128), 1)
    o_ref[0] = jnp.where(lane < 64, o[:128], pltpu.roll(o[128:], 64, 1)).astype(BF)


MINE = pl.BlockSpec((128, 128), lambda j, s: (2 * j + s[0], 0))


def block3(n, m):
    return pl.BlockSpec((1, n, m), lambda j, s: (j, 0, 0))


def attend(marks, q0, q1, k, v):
    return pl.pallas_call(
        attend_kernel,
        grid_spec=pltpu.PrefetchScalarGridSpec(
            num_scalar_prefetch=1,
            grid=(8,),
            in_specs=[MINE, MINE, whole(GROUP, 128), whole(GROUP, 128)],
            out_specs=[block3(128, 128), block3(256, 1)],
        ),
        out_shape=[sds((8, 128, 128), BF), sds((8, 256, 1), F32)],
        compiler_params=params(),
        name="attend",
    )(marks, q0, q1, k, v)


def three(v):
    hi = v.astype(BF).astype(F32)
    mid = (v - hi).astype(BF).astype(F32)
    return hi, mid, v - hi - mid


def attend_back_kernel(s_ref, q0_ref, q1_ref, k_ref, v_ref, o_ref, l_ref, g_ref,
                       dq_ref, own_ref, other_ref, dk_ref, dv_ref):
    @pl.when(pl.program_id(0) == 0)
    def _():
        dk_ref[...] = jnp.zeros_like(dk_ref)
        dv_ref[...] = jnp.zeros_like(dv_ref)

    lane = lax.broadcasted_iota(jnp.int32, (256, 128), 1)
    q = jnp.concatenate([q0_ref[...], q1_ref[...]], 0)
    h0, h1, h2 = three(l_ref[0])
    ql = jnp.where(lane == 68, -h0, jnp.where(lane == 69, -h1, jnp.where(lane == 70, -h2, q.astype(F32))))
    ql = ql.astype(BF)
    g = g_ref[0].astype(F32)
    o = o_ref[0].astype(F32)
    g = jnp.concatenate([g, pltpu.roll(g, 64, 1)], 0)
    o = jnp.concatenate([o, pltpu.roll(o, 64, 1)], 0)
    g = jnp.where(lane < 64, g, 0.0)
    centre = jnp.sum(g * o, axis=1, keepdims=True)
    c0, c1, c2 = three(centre)
    gl = jnp.where(lane == 64, -c0, jnp.where(lane == 65, -c1, jnp.where(lane == 66, -c2, g)))
    gl = gl.astype(BF)
    gb = g.astype(BF)
    dq = jnp.zeros((256, 128), F32)
    for j in range(GROUP // CHUNK):
        rows = pl.ds(j * CHUNK, CHUNK)
        k = k_ref[rows, :]
        st = dot(k, ql, NT)
        pt = jnp.exp2(st)
        gt = dot(v_ref[rows, :], gl, NT)
        ds = (pt * gt).astype(BF)
        dv_ref[rows, :] += dot(pt.astype(BF), gb)
        dk_ref[rows, :] += dot(ds, q)
        dq = dq + dot(ds, k, TN)
    dq_ref[0] = dq

    @pl.when(pl.program_id(0) == 7)
    def _():
        core = s_ref[0]
        low = lax.broadcasted_iota(jnp.int32, (128, 128), 1) < 64

        def block(j, c):
            rows = pl.ds(pl.multiple_of((2 * j + c) * 128, 128), 128)
            return jnp.where(low, dk_ref[rows, :] * LN2, pltpu.roll(dv_ref[rows, :], 64, 1))

        for j in range(8):
            own_ref[j] = block(j, core)
            other_ref[j] = block(j, 1 - core).astype(BF)


def attend_back(marks, q0, q1, k, v, o, l, g):
    return pl.pallas_call(
        attend_back_kernel,
        grid_spec=pltpu.PrefetchScalarGridSpec(
            num_scalar_prefetch=1,
            grid=(8,),
            in_specs=[MINE, MINE, whole(GROUP, 128), whole(GROUP, 128), block3(128, 128), block3(256, 1),
                      block3(128, 128)],
            out_specs=[block3(256, 128), whole(8, 128, 128), whole(8, 128, 128)],
            scratch_shapes=[pltpu.VMEM((GROUP, 128), F32)] * 2,
        ),
        out_shape=[sds((8, 256, 128), F32), sds((8, 128, 128), F32), sds((8, 128, 128), BF)],
        compiler_params=params(),
        name="attend_back",
    )(marks, q0, q1, k, v, o, l, g)


def heads_back_kernel(s_ref, dq_ref, own_ref, got_ref, raw_ref, f_ref, g_ref, c_ref, sin_ref, bd_ref,
                      out_ref, scaled_ref, gain_ref):
    @pl.when(pl.program_id(0) == 0)
    def _():
        gain_ref[...] = jnp.zeros_like(gain_ref)

    lane1 = lax.broadcasted_iota(jnp.int32, (128, 128), 1)
    dq = dq_ref[0] * HEAD**-0.5
    dq = jnp.where(lane1 < 64, dq[:128], pltpu.roll(dq[128:], 64, 1))
    d = jnp.concatenate([dq, own_ref[0] + got_ref[0].astype(F32)], 1)
    raw = raw_ref[...]
    lane = lax.broadcasted_iota(jnp.int32, (128, 256), 1)
    bd = bd_ref[...]
    fac = jnp.where(lane < 192, lax.rsqrt(exact_sums(raw * raw, bd) + EPS_HEAD), 1.0)
    hat = raw * fac
    c, s = wide_tables(c_ref[...], sin_ref[...], lane)
    dh = d * c - half_turn(d * s, lane)
    gain_ref[...] += jnp.sum(dh * hat, axis=0, keepdims=True)
    dn = dh * g_ref[...]
    back = fac * (dn - hat * exact_sums(dn * hat, bd))
    res = jnp.where(lane < 192, back, d)
    out_ref[0] = res.astype(BF)
    scaled_ref[...] = (res * f_ref[...]).astype(BF)


def heads_back(marks, dq, own, got, raw, f, gains, cos, sin):
    mine = lambda m: pl.BlockSpec((128, m), lambda j, s: (2 * j + s[0], 0))
    return pl.pallas_call(
        heads_back_kernel,
        grid_spec=pltpu.PrefetchScalarGridSpec(
            num_scalar_prefetch=1,
            grid=(8,),
            in_specs=[block3(256, 128), block3(128, 128), block3(128, 128), mine(256), mine(1), whole(1, 256),
                      mine(128), mine(128), whole(256, 256)],
            out_specs=[block3(128, 256), pl.BlockSpec((128, 256), lambda j, s: (j, 0)), whole(1, 256)],
        ),
        out_shape=[sds((8, 128, 256), BF), sds((PLANE, 256), BF), sds((1, 256), F32)],
        compiler_params=params(),
        name="heads_back",
    )(marks, dq, own, got, raw, f, gains, cos, sin, head_sums())


def norm_factor(v):
    return lax.rsqrt(jnp.mean(v * v, axis=1, keepdims=True) + EPS_WIDE)


def after_attention_kernel(s_ref, j_ref, *refs):
    own, sib = refs[0:4], refs[4]
    x_ref, g_ref, hidden_ref, middle_ref, w_ref = refs[5:]
    core, a, b = s_ref[0], s_ref[1], s_ref[2]
    for i, d in enumerate((1, 3, 2, 0)):
        for r in range(2):
            chip = ((a - d) & 3) * 2 + (b ^ (1 - r))
            at = chip * 128 + core * 64
            w_ref[pl.ds(pl.multiple_of(at, 64), 64), :] = own[i][r]
            at = chip * 128 + (1 - core) * 64
            w_ref[pl.ds(pl.multiple_of(at, 64), 64), :] = sib[i, r]
    hidden = x_ref[...].astype(F32)
    for j in range(8):
        hidden = hidden + dot(j_ref[j], w_ref[j * 128 : j * 128 + 128, :])
    hidden_ref[...] = hidden
    middle_ref[...] = (hidden * norm_factor(hidden) * g_ref[...]).astype(BF)


def after_attention(marks, joined, own, sib, x, gain):
    return pl.pallas_call(
        after_attention_kernel,
        grid_spec=pltpu.PrefetchScalarGridSpec(
            num_scalar_prefetch=1,
            grid=(1,),
            in_specs=[whole(8, 128, 128)] + [whole(2, 64, D)] * 4 + [whole(4, 2, 64, D), whole(128, D), whole(1, D)],
            out_specs=[whole(128, D), whole(128, D), whole(D, D)],
        ),
        out_shape=[sds((128, D), F32), sds((128, D), BF), sds((D, D), BF)],
        compiler_params=params(),
        name="after_attention",
    )(marks, joined, *own, sib, x, gain)


def second_back_kernel(a0, a1, a2, a3, b0, b1, hidden_ref, cot_ref, g_ref, w_ref,
                       grad_ref, low_ref, joined_ref, gain_ref):
    fa = a0[...].astype(F32) + a1[...].astype(F32) + a2[...].astype(F32) + a3[...].astype(F32)
    fb = b0[...].astype(F32) + b1[...].astype(F32)
    mg = jnp.concatenate([fa, fb], 0)
    hidden = hidden_ref[...]
    f = norm_factor(hidden)
    hat = hidden * f
    gain_ref[...] = jnp.sum(mg * hat, axis=0, keepdims=True)
    dn = mg * g_ref[...]
    grad = cot_ref[...].astype(F32) + f * (dn - hat * jnp.mean(dn * hat, axis=1, keepdims=True))
    grad_ref[...] = grad
    low = grad.astype(BF)
    low_ref[...] = low
    joined = dot(low, w_ref[...], NT).astype(BF)
    for j in range(8):
        joined_ref[j] = joined[:, j * 128 : j * 128 + 128]


def second_back(terms_a, terms_b, hidden, cot, gain, w):
    return pl.pallas_call(
        second_back_kernel,
        out_shape=[sds((128, D), F32), sds((128, D), BF), sds((8, 128, 128), BF), sds((1, D), F32)],
        compiler_params=params(),
        name="second_back",
    )(*terms_a, *terms_b, hidden, cot, gain, w)


def first_back_kernel(raw_ref, w_ref, x_ref, g_ref, grad_ref, out_ref):
    ng = dot(raw_ref[0], w_ref[0:256, :])
    for j in range(1, 8):
        ng = ng + dot(raw_ref[j], w_ref[j * 256 : j * 256 + 256, :])
    x = x_ref[...].astype(F32)
    f = norm_factor(x)
    hat = x * f
    dn = ng * g_ref[...]
    out_ref[...] = (grad_ref[...] + f * (dn - hat * jnp.mean(dn * hat, axis=1, keepdims=True))).astype(BF)


def first_back(raw, w, x, gain, grad):
    return pl.pallas_call(
        first_back_kernel,
        out_shape=sds((128, D), BF),
        compiler_params=params(),
        name="first_back",
    )(raw, w, x, gain, grad)


def place_experts_kernel(s_ref, *refs):
    ya, xb, out = refs[0:4], refs[4:6], refs[6]
    a, b = s_ref[3], s_ref[4]
    for i, d in enumerate((1, 3, 2, 0)):
        for r in range(2):
            block = ((a - d) & 3) * 2 + (b ^ (1 - r))
            at = block * 128
            out[pl.ds(pl.multiple_of(at, 64), 64), :] = ya[i][r]
            at = block * 128 + 64
            out[pl.ds(pl.multiple_of(at, 64), 64), :] = xb[r][i]


def place_experts(marks, ya, xb):
    m = ya[0].shape[2]
    return pl.pallas_call(
        place_experts_kernel,
        grid_spec=pltpu.PrefetchScalarGridSpec(
            num_scalar_prefetch=1,
            grid=(1,),
            in_specs=[whole(2, 64, m)] * 4 + [whole(4, 64, m)] * 2,
            out_specs=whole(D, m),
        ),
        out_shape=sds((D, m), BF),
        compiler_params=params(),
        name="place_experts",
    )(marks, *ya, *xb)


def experts_kernel(s_ref, mid_ref, up_ref, g_ref, w_ref, entry_ref, gg_ref, ug_ref, in_ref):
    mid = mid_ref[...].reshape(256, D)
    up = up_ref[...].reshape(256, D)
    gates = g_ref[...].reshape(256, 2)
    entry = None
    for e in range(2):
        cg = slice(e * FF, e * FF + FF)
        cu = slice(1024 + e * FF, 1024 + e * FF + FF)
        cd = slice(2048 + e * FF, 2048 + e * FF + FF)
        gp = dot(mid, w_ref[:, cg])
        u = dot(mid, w_ref[:, cu])
        g = gates[:, e : e + 1]
        ig = dot(up, w_ref[:, cd]) * g
        sig = 0.5 * jnp.tanh(0.5 * gp) + 0.5
        act = gp * sig
        inner = (g * act * u).astype(BF)
        gg = (ig * u * (sig + act * (1.0 - sig))).astype(BF)
        ug = (ig * act).astype(BF)
        part = dot(gg, w_ref[:, cg], NT) + dot(ug, w_ref[:, cu], NT)
        entry = part if entry is None else entry + part
        for ref, v in ((in_ref, inner), (gg_ref, gg), (ug_ref, ug)):
            ref[0, :, :, e * FF : e * FF + FF] = v.reshape(2, 128, FF)
    entry = entry.astype(BF)
    own = s_ref[2]
    entry_ref[0, own ^ 1 ^ 0 ^ 0] = entry[:128]
    entry_ref[0, own] = entry[128:]


def run_experts(marks, which, mid, up, gates, w):
    def group(m):
        return pl.BlockSpec((1, 2, 1, 128, m), lambda i, s: (s[8 + i], 0, s[which], 0, 0))

    hid = pl.BlockSpec((1, 2, 128, 2 * FF), lambda i, s: (s[8 + i], 0, 0, 0))
    entry = pl.BlockSpec((1, 2, 128, D), lambda i, s: (i, 0, 0, 0))
    return pl.pallas_call(
        experts_kernel,
        grid_spec=pltpu.PrefetchScalarGridSpec(
            num_scalar_prefetch=1,
            grid=(4,),
            in_specs=[group(D), group(D), group(2), whole(D, 6 * FF)],
            out_specs=[entry, hid, hid, hid],
        ),
        out_shape=[sds((4, 2, 128, D), BF)] * 4,
        compiler_params=params(),
        name="run_experts",
    )(marks, mid, up, gates, w)


def results_kernel(s_ref, own_ref, other_ref, w_ref, out_ref):
    core = s_ref[0]
    w = w_ref[...]
    out_ref[0, :, core] = dot(own_ref[...].reshape(256, 2 * FF), w, NT).astype(BF).reshape(2, 128, D)
    out_ref[0, :, 1 - core] = dot(other_ref[...].reshape(256, 2 * FF), w, NT).astype(BF).reshape(2, 128, D)


def results(marks, own, other, w):
    hid = pl.BlockSpec((1, 2, 128, 2 * FF), lambda i, s: (i, 0, 0, 0))
    return pl.pallas_call(
        results_kernel,
        grid_spec=pltpu.PrefetchScalarGridSpec(
            num_scalar_prefetch=1,
            grid=(4,),
            in_specs=[hid, hid, pl.BlockSpec((D, 2 * FF), lambda i, s: (0, 2))],
            out_specs=pl.BlockSpec((1, 2, 2, 128, D), lambda i, s: (i, 0, 0, 0, 0)),
        ),
        out_shape=sds((4, 2, 2, 128, D), BF),
        compiler_params=params(),
        name="results",
    )(marks, own, other, w)


def weights_kernel(s_ref, m0, m1, u0, u1, gg0, gg1, ug0, ug1, in0, in1,
                   send_ref, keep_ref, b1_ref, b3_ref, b2_ref, b0_ref):
    i = pl.program_id(0)
    b = s_ref[4]
    sides = [m0[...].reshape(PLANE, 256), m1[...].reshape(PLANE, 256),
             u0[...].reshape(PLANE, 256), u1[...].reshape(PLANE, 256)]
    sides = [v.T for v in sides]
    for n, (l0, l1, r0, r1) in enumerate((
        (sides[0], sides[1], gg0, gg1),
        (sides[0], sides[1], ug0, ug1),
        (sides[2], sides[3], in0, in1),
    )):
        cols = slice(n * 1024, n * 1024 + 1024)
        o = dot(l0, r0[...].reshape(PLANE, 1024)) + dot(l1, r1[...].reshape(PLANE, 1024))
        o = o.astype(BF)
        other = jnp.where(b == 0, o[128:], o[:128])
        own = jnp.where(b == 0, o[:128], o[128:])
        send_ref[0, :, cols] = other[:64]
        keep_ref[0, :, cols] = own[:64]
        for k, ref in enumerate((b1_ref, b3_ref, b2_ref, b0_ref)):
            @pl.when(i == k)
            def _():
                ref[0, :, cols] = other[64:]
                ref[1, :, cols] = own[64:]


def weight_grads(marks, mid, up, gg, ug, inner):
    def side(which):
        return pl.BlockSpec((4, 2, 1, 128, 256), lambda i, s: (0, 0, s[which], 0, s[12 + i]))

    hid = whole(4, 2, 128, 2 * FF)
    part = pl.BlockSpec((1, 64, 6 * FF), lambda i, s: (i, 0, 0))
    return pl.pallas_call(
        weights_kernel,
        grid_spec=pltpu.PrefetchScalarGridSpec(
            num_scalar_prefetch=1,
            grid=(4,),
            in_specs=[side(0), side(5), side(0), side(5)] + [hid] * 6,
            out_specs=[part, part] + [whole(2, 64, 6 * FF)] * 4,
        ),
        out_shape=[sds((4, 64, 6 * FF), BF)] * 2 + [sds((2, 64, 6 * FF), BF)] * 4,
        compiler_params=params(58),
        name="weight_grads",
    )(marks, mid, mid, up, up, *gg, *ug, *inner)


def qkv_grads_kernel(s_ref, x_ref, r_ref, w_ref, g_ref, own_ref, other_ref, first_ref):
    core = s_ref[0]
    o = dot(x_ref[...].reshape(PLANE, 256), r_ref[...], TN)
    first_ref[...] = jnp.sum(o * w_ref[...].astype(F32), axis=1, keepdims=True)
    o = o * g_ref[...]
    own_ref[...] = jnp.where(core == 0, o[:, :128], o[:, 128:])
    other_ref[...] = jnp.where(core == 0, o[:, 128:], o[:, :128]).astype(BF)


def qkv_grads(marks, x, r, w, gain):
    rows = lambda m: pl.BlockSpec((256, m), lambda i, s: (i, 0))
    return pl.pallas_call(
        qkv_grads_kernel,
        grid_spec=pltpu.PrefetchScalarGridSpec(
            num_scalar_prefetch=1,
            grid=(4,),
            in_specs=[pl.BlockSpec((4, 2, 1, 128, 256), lambda i, s: (0, 0, s[0], 0, i)), whole(PLANE, 256),
                      rows(256), rows(1)],
            out_specs=[rows(128), rows(128), rows(1)],
        ),
        out_shape=[sds((D, 128), F32), sds((D, 128), BF), sds((D, 1), F32)],
        compiler_params=params(),
        name="qkv_grads",
    )(marks, x, r, w, gain)


def out_grads_kernel(s_ref, h0, h1, h2, h3, j_ref, own_ref, other_ref):
    core, a, b = s_ref[0], s_ref[1], s_ref[2]
    acc = jnp.zeros((D, 128), F32)
    for ref, d in zip((h0, h1, h2, h3), (1, 3, 2, 0)):
        at = ((a - d) & 3) * 2
        both = jnp.concatenate([j_ref[at + (b ^ 1)], j_ref[at + b]], 0)
        acc = acc + dot(ref[...].reshape(256, D), both, TN)
    other = pltpu.roll(acc, 64, 1)
    own_ref[...] = jnp.where(core == 0, acc, other)[:, :64]
    other_ref[...] = jnp.where(core == 0, other, acc)[:, :64].astype(BF)


def out_grads(marks, pieces, joined):
    return pl.pallas_call(
        out_grads_kernel,
        grid_spec=pltpu.PrefetchScalarGridSpec(
            num_scalar_prefetch=1,
            grid=(1,),
            in_specs=[whole(2, 128, D)] * 4 + [whole(8, 128, 128)],
            out_specs=[whole(D, 64), whole(D, 64)],
        ),
        out_shape=[sds((D, 64), F32), sds((D, 64), BF)],
        compiler_params=params(),
        name="out_grads",
    )(marks, *pieces, joined)


def body(tokens, cotangent, deal_order, lengths, routes, route_gates, gain_first, gain_second, gain_query, gain_key,
         weight_qkv, weight_out, weight_gate, weight_up, weight_down):
    col = lax.axis_index("col")
    core = col % 2
    a, b = place("col")
    ra, rb = place("row")
    order = [(a + d) % 4 for d in (1, 3, 2, 0)]
    row_order = [(ra + d) % 4 for d in (1, 3, 2, 0)]
    marks = jnp.stack([core, a, b, ra, rb, 1 - core, core, core] + order + row_order).astype(jnp.int32)
    planes = [[i for i in range(16) if i % 2 == k] for k in range(2)]
    swap_all = partial(lax.all_to_all, axis_name="col", split_axis=0, concat_axis=0, tiled=True,
                       axis_index_groups=planes)

    x_all = lax.all_gather(tokens, "col", axis=0, tiled=True)

    small = jnp.concatenate([weight_qkv, weight_out], 1).astype(BF)
    wide = jnp.concatenate([w.reshape(128, 2 * FF) for w in (weight_gate, weight_up, weight_down)], 1).astype(BF)
    pieces = gather_plain(small, "row")
    wide_a, wide_b = gather_first(wide, "row")
    small = jnp.zeros((4, 2, 128, 192), BF)
    for d, piece in zip((1, 3, 2, 0), pieces):
        small = lax.dynamic_update_slice(small, jnp.where(rb == 0, piece[::-1], piece)[None], ((ra - d) % 4, 0, 0, 0))
    small = small.reshape(D, 192)
    w_own = small[:, :128]
    w_pair = step_core(w_own)
    w_chip = jnp.where(core == 0, jnp.concatenate([w_own, w_pair], 1), jnp.concatenate([w_pair, w_own], 1))
    own_t = small.T
    out_own = gather_plain(own_t[128:], "col")
    out_sib = step_core(jnp.stack(out_own))
    x_all, cotangent_late, wide_a, wide_b, out_sib_late = together(x_all, cotangent, wide_a, wide_b, out_sib)
    wide_ya, wide_xb = gather_second(wide_a, wide_b, "row")

    deal_row = deal_order[0]
    slots = jnp.arange(GROUP, dtype=jnp.int32)
    inverse = jnp.zeros((GROUP,), jnp.int32).at[deal_row].set(slots)
    finish = jnp.cumsum(lengths[0])
    starts = finish - lengths[0]
    segment = jnp.sum((inverse[:, None] >= finish[None, :]).astype(jnp.int32), axis=1)
    labels = jnp.arange(4, dtype=jnp.int32)
    anchor = jnp.sum(jnp.where(segment[:, None] == labels[None, :], starts[None, :], 0), axis=1)
    offset = (inverse - anchor).astype(F32)
    frequency = THETA ** (-(jnp.arange(128) % 32).astype(F32) * 2.0 / HEAD)
    angles = offset[:, None] * frequency[None, :]
    cos, sin = jnp.cos(angles), jnp.sin(angles)

    r16 = routes.astype(BF)
    g_hi, g_mid, g_lo = three(route_gates)
    extra = jnp.concatenate([r16, g_hi.astype(BF), g_mid.astype(BF), g_lo.astype(BF)], 1).reshape(4, 1024)
    extra = jnp.concatenate([extra, jnp.zeros((12, 1024), BF)], 0)
    cot_all = lax.all_gather(jnp.concatenate([cotangent_late, extra], 0), "col", axis=0, tiled=False)
    cot_all = cot_all.reshape(4, 2, 2, 144, D)
    info = cot_all[:, :, :, 128:132].reshape(GROUP, 32).astype(F32)
    names = info[:, :8]
    values = info[:, 8:16] + info[:, 16:24] + info[:, 24:32]
    mine = (col * 2 + jnp.arange(2)).astype(F32)
    gates = jnp.sum(jnp.where(names[:, None, :] == mine[None, :, None], values[:, None, :], 0.0), axis=2)
    gates = gates[inverse].reshape(4, 2, 2, 128, 2)

    gains = jnp.concatenate([gain_query, gain_query, gain_key, jnp.ones((HEAD,), F32)])[None, :]
    w_scaled = (gain_first[:, None] * w_chip.astype(F32)).astype(BF)
    q0, q1, k, v, raw, f1_all = project_heads(x_all, w_scaled, gains, cos, sin, segment[:, None])
    joined, logs = attend(marks, q0, q1, k, v)
    hidden, middle, wout_t = after_attention(marks, swap_all(joined), out_own, out_sib, tokens, gain_second[None])
    mid_all = lax.all_gather(middle, "col", axis=0, tiled=True).reshape(4, 2, 2, 128, D)
    own_t, middle_late = together(own_t, mid_all)
    wqkv_t = lax.all_gather(own_t[:128], "col", axis=0, tiled=True)

    w_all = place_experts(marks, wide_ya, wide_xb)
    e_other, gg1, ug1, in1 = run_experts(marks, 5, mid_all, cot_all, gates, w_all)
    e_got = step_core(e_other)
    e_own, gg0, ug0, in0 = run_experts(marks, 0, mid_all, cot_all, gates, w_all)

    def entry(i, r, h):
        rows = slice(h * 64, h * 64 + 64)
        return (e_own[i, r, rows].astype(F32) + e_got[i, r, rows].astype(F32)).astype(BF)

    def entries(h, r, items):
        rows = slice(h * 64, h * 64 + 64)
        return (e_own[items, r, rows].astype(F32) + e_got[items, r, rows].astype(F32)).astype(BF)

    terms_a, terms_b = scatter_pieces(
        entries(0, 0, slice(0, 4)), entries(0, 1, slice(0, 4)),
        [entries(1, slice(0, 2), i) for i in range(4)], "col")
    out_parts = results(marks, in0, in1, w_all).reshape(GROUP, D)
    out_sum = lax.psum_scatter(out_parts, "col", scatter_dimension=0, tiled=True).astype(F32)
    block_out = (hidden + out_sum).astype(BF)
    send_a, keep_a, *send_b = weight_grads(marks, mid_all, cot_all, (gg0, gg1), (ug0, ug1), (in0, in1))
    wide_a, wide_b = scatter_pieces(send_a, keep_a, send_b, "row")
    grads_w = jnp.concatenate([added(wide_a), added(wide_b)], 0)

    hidden_grad, hidden_low, joined_grad, second = second_back(
        terms_a, terms_b, hidden, cotangent, gain_second[None], wout_t)
    joined_grad = swap_all(joined_grad)
    hidden_pieces = gather_plain(hidden_low, "col")
    dq, dkv_own, dkv_other = attend_back(marks, q0, q1, k, v, joined, logs, joined_grad)
    dkv_got = step_core(dkv_other)
    raw_grad, raw_scaled, gain_heads = heads_back(marks, dq, dkv_own, dkv_got, raw, f1_all, gains, cos, sin)
    raw_got = swap_all(raw_grad)
    own_q, other_q, first = qkv_grads(marks, x_all.reshape(4, 2, 2, 128, D), raw_scaled, w_chip, gain_first[:, None])
    own_o, other_o = out_grads(marks, hidden_pieces, joined)
    got = step_core(jnp.concatenate([other_q, other_o], 1))
    own = jnp.concatenate([own_q, own_o], 1) + got.astype(F32)
    own = own.astype(BF).reshape(4, 2, 128, 192)
    other_b = lax.dynamic_index_in_dim(own, 1 - rb, 1, keepdims=False)
    own_b = lax.dynamic_index_in_dim(own, rb, 1, keepdims=False)
    own = (own_b.astype(F32) + step_pair(other_b, "row").astype(F32)).astype(BF)
    terms = [step_ring(lax.dynamic_index_in_dim(own, (ra + d) % 4, 0, keepdims=False), "row", d) for d in AHEAD]
    own = added(terms + [lax.dynamic_index_in_dim(own, ra, 0, keepdims=False)])

    input_grad = first_back(raw_got, wqkv_t, tokens, gain_first[None], hidden_grad)

    heads = gain_heads[0]
    packed = jnp.concatenate([first[:, 0], second[0], heads[:64] + heads[64:128], heads[128:192]]).reshape(17, 128)
    packed = sum_all(packed).reshape(-1)
    shape = (128, 2, FF)
    return (
        block_out,
        input_grad,
        packed[:1024],
        packed[1024:2048],
        packed[2048:2112],
        packed[2112:],
        own[:, :128],
        own[:, 128:],
        grads_w[:, :1024].reshape(shape),
        grads_w[:, 1024:2048].reshape(shape),
        grads_w[:, 2048:].reshape(shape),
    )


def solution(mesh):
    both = P(("row", "col"), None)
    return jax.shard_map(
        body,
        mesh=mesh,
        in_specs=(both, both, P("row", None), P("row", None), both, both, P(), P(), P(), P(),
                  P("row", "col"), P("row", "col"), P("row", "col", None), P("row", "col", None),
                  P("row", "col", None)),
        out_specs=(both, both, P(), P(), P(), P(), P("row", "col"), P("row", "col"), P("row", "col", None),
                   P("row", "col", None), P("row", "col", None)),
        check_vma=False,
    )
```

time: 1120 us -> 580 us (0.52)
  waiting for transfers between devices: 635 us -> 216 us
  Pallas kernels: 0 us -> 126 us
  blocking collectives: 123 us -> 0 us
  matrix products: 96.3 us -> 0 us
  local copies, waits for them, and re-layouts: 129 us -> 80.1 us
  starting transfers between devices: 50.2 us -> 95.3 us
  other arithmetic: 54.5 us -> 38.6 us
    reduce_scatter x4 -> x1, waiting for transfers between devices: 186 us -> 0.01 us  [body(): lax.psum_scatter(out_parts, 'col', scatter_dimension=0, tiled=True)]
    all_to_all x8 -> x3, waiting for transfers between devices: 179 us -> 2.01 us  [the longest x1 2.01 us: body(): joined_grad = swap_all(joined_grad)]
    ppermute x2 -> x52, waiting for transfers between devices: 1.62 us -> 178 us  [the longest x10 88.5 us: step_pair(): return lax.ppermute(v, axis, route)]
    unnamed x15 -> x5, waiting for transfers between devices: 170 us -> 0.75 us
    pallas_call x0 -> x14, Pallas kernels: none -> 126 us  [the longest x2 34.5 us: run_experts(): pl.pallas_call(experts_kernel, grid_spec=pltpu.PrefetchScalarGridSpec(num...]
    dot_general x43 -> x0, matrix products: 96.3 us -> none  [the longest x1 10.6 us: body(): jnp.einsum('nemd,def->nemf', expert_grad, full_down, preferred_element_ty...]
    ppermute x2 -> x52, starting transfers between devices: 0.72 us -> 77.1 us  [the longest x30 39.1 us: step_ring(): return lax.ppermute(v, axis, route)]
    psum x1 -> x0, blocking collectives: 66.3 us -> none  [body(): lax.psum((first_gain, second_gain, query_gain, key_gain), ('row', 'col'))]
  transfers between devices with their start and end apart: 22 -> 60, of which waited for: 14 -> 27; matrix products, arithmetic and copies ran while one was open for 13% -> 15% of each run, Pallas kernels for 0% -> 19%
where the time goes in v1:
time: 580 us; the launch traced here: 572 us
  waiting for transfers between devices  216 us (37%)
  Pallas kernels  126 us (22%)
  starting transfers between devices  95.3 us (16%)
  local copies, waits for them, and re-layouts  80.1 us (14%)
  other arithmetic  38.6 us (7%)
  between operations  15.3 us (3%)
    ppermute x10, waiting for transfers between devices, step_pair(): return lax.ppermute(v, axis, route)  88.5 us
    ppermute x30, waiting for transfers between devices, step_ring(): return lax.ppermute(v, axis, route)  84.8 us
    ppermute x30, starting transfers between devices, step_ring(): return lax.ppermute(v, axis, route)  39.1 us
    all_gather x1, waiting for transfers between devices, body(): lax.all_gather(middle, 'col', axis=0, tiled=True).reshape(4, 2, 2, 128, D)  35.2 us
    pallas_call x2, Pallas kernels, run_experts(): pl.pallas_call(experts_kernel, grid_spec=pltpu.PrefetchScalarGridSpec(num...  34.5 us
    unnamed x137, local copies, waits for them, and re-layouts  31.4 us
    pallas_call x1, Pallas kernels, weight_grads(): pl.pallas_call(weights_kernel, grid_spec=pltpu.PrefetchScalarGridSpec(num...  23.8 us
    ppermute x10, starting transfers between devices, step_pair(): return lax.ppermute(v, axis, route)  18 us
  transfers between devices with their start and end apart: 60, of which 27 were waited for; matrix products, arithmetic and copies ran while one was open for 15% of the time, Pallas kernels for 19%

profile of v1, /device:TPU:1, one launch (start us, length us, event | category | flops | bytes accessed | tf_op | source)
XLA Modules:
  0.0 571.9 jit_solution(1751236933355919301)
XLA Ops:
  12.0 2.5 collective-permute-start.1
  18.1 2.8 collective-permute-start.4
  23.6 8.0 %scatter_custom_fusion = s32[2048]{0:T(1024)S(1)} fusion(s32[2048]{0:T(1024)S(1)} %bitcast.219, s32[2048]{0:T(1024)S(1)} %iota.17, s32[]{:T(128)} %constant.159.clone.1), kind=kCustom, calls=%fused_computation.114 | custom fusion | bytes 8196 | tf_op jit(solution)/shard_map/scatter | solution.py:687
  33.7 2.6 collective-permute-done.5
  38.3 3.3 collective-permute-done.7
  44.0 7.8 %collective-permute-done.8 = bf16[64,1024]{0,1:T(8,128)(2,1)S(1)} collective-permute-done((bf16[64,1024]{0,1:T(8,128)(2,1)S(1)}, bf16[64,1024]{0,1:T(8,128)(2,1)S(1)}, u32[]{:S(2)}, u32[]{:S(2)}) %collective-permute-start.8) | collective-permute-done | bytes 131104 | tf_op jit(solution)/shard_map/ppermute | solution.py:63
  53.9 12.0 %collective-permute-done.11 = bf16[2,64,1024]{1,2,0:T(8,128)(2,1)S(1)} collective-permute-done((bf16[2,64,1024]{1,2,0:T(8,128)(2,1)S(1)}, bf16[2,64,1024]{1,2,0:T(8,128)(2,1)S(1)}, u32[]{:S(2)}, u32[]{:S(2)}) %collective-permute-start.11) | collective-permute-done | bytes 262176 | tf_op jit(solution)/shard_map/ppermute | solution.py:71
  67.9 7.9 %collective-permute-done.10 = bf16[2,64,1024]{1,2,0:T(8,128)(2,1)S(1)} collective-permute-done((bf16[2,64,1024]{1,2,0:T(8,128)(2,1)S(1)}, bf16[2,64,1024]{1,2,0:T(8,128)(2,1)S(1)}, u32[]{:S(2)}, u32[]{:S(2)}) %collective-permute-start.10) | collective-permute-done | bytes 262176 | tf_op jit(solution)/shard_map/ppermute | solution.py:71
  78.0 3.7 multiply_sine_fusion
  83.3 7.1 %collective-permute-done.9 = bf16[2,64,1024]{1,2,0:T(8,128)(2,1)} collective-permute-done((bf16[2,64,1024]{1,2,0:T(8,128)(2,1)S(1)}, bf16[2,64,1024]{1,2,0:T(8,128)(2,1)}, u32[]{:S(2)}, u32[]{:S(2)}) %collective-permute-start.9) | collective-permute-done | bytes 262176 | tf_op jit(solution)/shard_map/ppermute | solution.py:71
  90.4 3.4 pad_maximum_fusion
  93.8 2.7 copy.70
  99.1 2.7 pad_maximum_fusion.1.refs_5_
  106.2 7.8 %project_heads.1 = (bf16[2048,128]{1,0:T(8,128)(2,1)S(1)}, bf16[2048,128]{1,0:T(8,128)(2,1)S(1)}, bf16[2048,128]{1,0:T(8,128)(2,1)S(1)}, bf16[2048,128]{1,0:T(8,...) custom-call(bf16[2048,1024]{1,0:T(8,128)(2,1)} %all-gather.6.cloned.1.call-done.x_ref, ...), custom_call_target="tpu_custom_call" | custom-call | tf_op jit(solution)/shard_map/project_heads/pallas_call | solution.py:204
  115.0 10.0 %attend.1 = (bf16[8,128,128]{2,1,0:T(8,128)(2,1)}, f32[8,256,1]{2,1,0:T(8,128)S(1)}) custom-call(s32[16]{0:T(128)S(1)} %stack.125.s_ref, bf16[2048,128]{1,0:T(8,128)(2,1)S(1)} %get-tuple-element.73.q0_ref, bf16[2048,128]{1,0:T(8,128)(2,1)S(1)} %get-tuple-element.74.q1_ref, bf16[2048,128]{1,0:T(8,128)(2,1)S(1)} %get-tuple-element.75.k_ref, ...), custom_call_target="tpu_custom_call" | custom-call | tf_op jit(solution)/shard_map/attend/pallas_call | solution.py:242
  126.8 4.2 all-to-all-start
  142.2 2.4 after_attention.1
  151.2 35.2 %all-gather.8.cloned.1.call-done = bf16[2048,1024]{1,0:T(8,128)(2,1)} async-done(((bf16[128,1024]{1,0:T(8,128)(2,1)}), bf16[2048,1024]{1,0:T(8,128)(2,1)}) %all-gather.8.cloned.1.call-update) | async-done | bytes 4194320 | tf_op jit(solution)/shard_map/all_gather | solution.py:716
  188.1 2.5 collective-permute-start.17
  195.6 14.9 %collective-permute-done.14.refs_0_ = bf16[2,64,3072]{2,1,0:T(8,128)(2,1)} collective-permute-done((bf16[2,64,3072]{2,1,0:T(8,128)(2,1)S(1)}, bf16[2,64,3072]{2,1,0:T(8,128)(2,1)}, u32[]{:S(2)}, u32[]{:S(2)}) %collective-permute-start.14) | collective-permute-done | bytes 786464 | tf_op jit(solution)/shard_map/ppermute | solution.py:71
  210.5 18.0 %collective-permute-done.16.refs_2_ = bf16[2,64,3072]{2,1,0:T(8,128)(2,1)} collective-permute-done((bf16[2,64,3072]{2,1,0:T(8,128)(2,1)S(1)}, bf16[2,64,3072]{2,1,0:T(8,128)(2,1)}, u32[]{:S(2)}, u32[]{:S(2)}) %collective-permute-start.16) | collective-permute-done | bytes 786464 | tf_op jit(solution)/shard_map/ppermute | solution.py:71
  228.5 19.3 %collective-permute-done.17.refs_4_ = bf16[4,64,3072]{2,1,0:T(8,128)(2,1)} collective-permute-done((bf16[4,64,3072]{2,1,0:T(8,128)(2,1)}, bf16[4,64,3072]{2,1,0:T(8,128)(2,1)}, u32[]{:S(2)}, u32[]{:S(2)}) %collective-permute-start.17) | collective-permute-done | bytes 1572896 | tf_op jit(solution)/shard_map/ppermute | solution.py:63
  247.8 6.2 %place_experts.1.w_ref = bf16[1024,3072]{1,0:T(8,128)(2,1)} custom-call(s32[16]{0:T(128)S(1)} %stack.125.s_ref, bf16[2,64,3072]{2,1,0:T(8,128)(2,1)} %collective-permute-done.14.refs_0_, bf16[2,64,3072]{2,1,0:T(8,128)(2,1)} %collective-permute-done.15.refs_1_, bf16[2,64,3072]{2,1,0:T(8,128)(2,1)} %collective-permute-done.16.refs_2_, ...), custom_call_target="tpu_custom_call" | custom-call | tf_op jit(solution)/shard_map/place_experts/pallas_call | solution.py:469
  263.8 7.7 %gather_fusion = f32[2048,2]{1,0:T(8,128)S(1)} fusion(f32[2048,2]{1,0:T(8,128)} %copy.79, s32[2048]{0:T(1024)} %get-tuple-element.210), kind=kCustom, calls=%fused_computation | custom fusion | bytes 40960 | tf_op jit(solution)/shard_map/gather | solution.py:709
  271.5 17.5 %run_experts.3 = (bf16[4,2,128,1024]{3,2,1,0:T(8,128)(2,1)}, bf16[4,2,128,1024]{3,2,1,0:T(8,128)(2,1)S(1)}, bf16[4,2,128,1024]{3,2,1,0:T(8,128)(2,1)}, bf16[4,2,128,1024]{3,2,1,0:T(8,128)(2,1)}) custom-call(s32[16]{0:T(128)S(1)} %stack.125.s_ref, bf16[4,2,2,128,1024]{4,3,2,1,0:T(8,128)(2,1)} %bitcast.194, bf16[4,2,2,144,1024]{4,3,2,1,0:T(8,128)(2,1)} %bitcast.190, ...), custom_call_target="tpu_custom_call" | custom-call | tf_op jit(solution)/shard_map/run_experts/pallas_call | solution.py:517
  291.4 17.0 %run_experts.2 = (bf16[4,2,128,1024]{3,2,1,0:T(8,128)(2,1)S(1)}, bf16[4,2,128,1024]{3,2,1,0:T(8,128)(2,1)S(1)}, bf16[4,2,128,1024]{3,2,1,0:T(8,128)(2,1)}, bf16[4,2,128,1024]{3,2,1,0:T(8,128)(2,1)}) custom-call(s32[16]{0:T(128)S(1)} %stack.125.s_ref, bf16[4,2,2,128,1024]{4,3,2,1,0:T(8,128)(2,1)} %bitcast.195, bf16[4,2,2,144,1024]{4,3,2,1,0:T(8,128)(2,1)} %bitcast.191, ...), custom_call_target="tpu_custom_call" | custom-call | tf_op jit(solution)/shard_map/run_experts/pallas_call | solution.py:517
  309.7 2.3 copy-done.2
  312.1 8.4 %results.1 = bf16[4,2,2,128,1024]{4,3,2,1,0:T(8,128)(2,1)} custom-call(s32[16]{0:T(128)S(1)} %stack.125.s_ref, bf16[4,2,128,1024]{3,2,1,0:T(8,128)(2,1)S(1)} %copy-done.2, bf16[4,2,128,1024]{3,2,1,0:T(8,128)(2,1)S(1)} %copy-done.1, bf16[1024,3072]{1,0:T(8,128)(2,1)} %place_experts.1.w_ref), custom_call_target="tpu_custom_call" | custom-call | tf_op jit(solution)/shard_map/results/pallas_call | solution.py:540
  325.3 2.7 collective-permute-start.21
  328.1 23.8 %weight_grads.1 = (bf16[4,64,3072]{2,1,0:T(8,128)(2,1)}, bf16[4,64,3072]{2,1,0:T(8,128)(2,1)}, bf16[2,64,3072]{2,1,0:T(8,128)(2,1)}, bf16[2,64,3072]{2,1,0:T(8,1...) custom-call(s32[16]{0:T(128)} %copy-done.45, bf16[4,2,2,128,1024]{4,3,2,1,0:T(8,128)(2,1)} %bitcast.196, ...), custom_call_target="tpu_custom_call" | custom-call | tf_op jit(solution)/shard_map/weight_grads/pallas_call | solution.py:586
  352.0 2.6 collective-permute-start.44
  361.0 4.6 collective-permute-done.25.a2
  365.6 51.0 %collective-permute-done.26.b0 = bf16[64,1024]{1,0:T(8,128)(2,1)S(1)} collective-permute-done((bf16[64,1024]{1,0:T(8,128)(2,1)S(1)}, bf16[64,1024]{1,0:T(8,128)(2,1)S(1)}, u32[]{:S(2)}, u32[]{:S(2)}) %collective-permute-start.26) | collective-permute-done | bytes 131104 | tf_op jit(solution)/shard_map/ppermute | solution.py:63
  420.5 4.1 all-to-all-start.1
  434.1 17.1 %attend_back.1 = (f32[8,256,128]{2,1,0:T(8,128)S(1)}, f32[8,128,128]{2,1,0:T(8,128)S(1)}, bf16[8,128,128]{2,1,0:T(8,128)(2,1)}) custom-call(s32[16]{0:T(128)S(1)} %copy-done.46, bf16[2048,128]{1,0:T(8,128)(2,1)S(1)} %copy-done.13, bf16[2048,128]{1,0:T(8,128)(2,1)S(1)} %copy-done.15, bf16[2048,128]{1,0:T(8,128)(2,1)S(1)} %copy-done.17, ...), custom_call_target="tpu_custom_call" | custom-call | tf_op jit(solution)/shard_map/attend_back/pallas_call | solution.py:312
  459.9 7.2 %heads_back.1 = (bf16[8,128,256]{2,1,0:T(8,128)(2,1)}, bf16[1024,256]{1,0:T(8,128)(2,1)S(1)}, f32[1,256]{1,0:T(1,128)S(1)}) custom-call(s32[16]{0:T(128)S(1)} %copy-done.46, f32[8,256,128]{2,1,0:T(8,128)S(1)} %copy-done.34, f32[8,128,128]{2,1,0:T(8,128)S(1)} %copy-done.39, bf16[8,128,128]{2,1,0:T(8,128)(2,1)S(1)} %collective-permute-done.27.got_ref, ...), custom_call_target="tpu_custom_call" | custom-call | tf_op jit(solution)/shard_map/heads_back/pallas_call | solution.py:355
  467.1 4.0 qkv_grads.1
  477.0 2.4 collective-permute-start.51
  486.4 2.9 collective-permute-start.50
  495.5 6.3 %collective-permute-done.37.h1 = bf16[2,128,1024]{2,1,0:T(8,128)(2,1)S(1)} collective-permute-done((bf16[2,128,1024]{2,1,0:T(8,128)(2,1)S(1)}, bf16[2,128,1024]{2,1,0:T(8,128)(2,1)S(1)}, u32[]{:S(2)}, u32[]{:S(2)}) %collective-permute-start.37) | collective-permute-done | bytes 524320 | tf_op jit(solution)/shard_map/ppermute | solution.py:71
  505.8 2.3 out_grads.1
  508.2 5.6 collective-permute-start.39
  515.2 2.9 collective-permute-start.34
  521.9 9.8 %all-to-all-start.2 = ((bf16[8,128,256]{2,1,0:T(8,128)(2,1)}), bf16[8,128,256]{2,1,0:T(8,128)(2,1)S(1)}, u32[]{:S(2)}, u32[]{:S(2)}) async-start(bf16[8,128,256]{2,1,0:T(8,128)(2,1)} %get-tuple-element.99), calls=%async_computation.3 | async-start | bytes 1048576 | tf_op jit(solution)/shard_map/all_to_all | solution.py:750
  535.5 8.3 %collective-permute-done.40 = bf16[4,128,192]{1,2,0:T(8,128)(2,1)S(1)} collective-permute-done((bf16[4,128,192]{1,2,0:T(8,128)(2,1)S(1)}, bf16[4,128,192]{1,2,0:T(8,128)(2,1)S(1)}, u32[]{:S(2)}, u32[]{:S(2)}) %collective-permute-start.40) | collective-permute-done | bytes 196640 | tf_op jit(solution)/shard_map/ppermute | solution.py:63
  544.2 3.3 collective-permute-start.42
  548.6 3.0 collective-permute-done.41
  553.0 6.5 %copy.80.w_ref = bf16[2048,1024]{1,0:T(8,128)(2,1)} copy(bf16[2048,1024]{0,1:T(8,128)(2,1)} %all-gather.10.cloned.1.call-done) | data formatting | bytes 8388608 | tf_op jit(solution)/shard_map/all_gather | solution.py:718
  (327 shorter events, 146.5 us)
Async XLA Ops:
  7.2 97.9 %all-gather.6.cloned.1.call-start = ((), (), s32[]{:S(2)}) async-start(), calls=%async_computation.4 | async-start | bytes 4456448 | tf_op jit(solution)/shard_map/all_gather | solution.py:666
  12.0 87.0 %collective-permute-start.1 = (bf16[64,3072]{1,0:T(8,128)(2,1)}, bf16[64,3072]{1,0:T(8,128)(2,1)}, u32[]{:S(2)}, u32[]{:S(2)}) collective-permute-start(bf16[64,3072]{1,0:T(8,128)(2,1)} %get-tuple-element.193), channel_id=1, source_target_pairs={{0,32},{16,48},{32,64},{48,80},{64,96},{80,112},{96,0},{112,16},{1... | collective-permute-start | bytes 1179656 | tf_op jit(solution)/shard_map/ppermute | solution.py:71
  14.5 84.6 %collective-permute-start.2 = (bf16[64,3072]{1,0:T(8,128)(2,1)}, bf16[64,3072]{1,0:T(8,128)(2,1)}, u32[]{:S(2)}, u32[]{:S(2)}) collective-permute-start(bf16[64,3072]{1,0:T(8,128)(2,1)} %get-tuple-element.193), channel_id=1, source_target_pairs={{0,96},{16,112},{32,0},{48,16},{64,32},{80,48},{96,64},{112,80},{1... | collective-permute-start | bytes 1179656 | tf_op jit(solution)/shard_map/ppermute | solution.py:71
  16.6 82.4 %collective-permute-start.3 = (bf16[64,3072]{1,0:T(8,128)(2,1)}, bf16[64,3072]{1,0:T(8,128)(2,1)}, u32[]{:S(2)}, u32[]{:S(2)}) collective-permute-start(bf16[64,3072]{1,0:T(8,128)(2,1)} %get-tuple-element.193), channel_id=1, source_target_pairs={{0,64},{16,80},{32,96},{48,112},{64,0},{80,16},{96,32},{112,48},{1... | collective-permute-start | bytes 1179656 | tf_op jit(solution)/shard_map/ppermute | solution.py:71
  22.8 13.4 %collective-permute-start.5 = (bf16[2,128,192]{2,1,0:T(8,128)(2,1)S(1)}, bf16[2,128,192]{2,1,0:T(8,128)(2,1)S(1)}, u32[]{:S(2)}, u32[]{:S(2)}) collective-permute-start(bf16[2,128,192]{2,1,0:T(8,128)(2,1)S(1)} %maximum_maximum_fusion.1), channel_id=1, source_target_pairs={{0,32},{16,48},{32,64},{48,80},{64,96},{80,112},{96,0},{112,16},{1... | collective-permute-start | bytes 294920 | tf_op jit(solution)/shard_map/ppermute | solution.py:71
  31.7 6.5 %collective-permute-start.6 = (bf16[2,128,192]{2,1,0:T(8,128)(2,1)S(1)}, bf16[2,128,192]{2,1,0:T(8,128)(2,1)S(1)}, u32[]{:S(2)}, u32[]{:S(2)}) collective-permute-start(bf16[2,128,192]{2,1,0:T(8,128)(2,1)S(1)} %maximum_maximum_fusion.1), channel_id=1, source_target_pairs={{0,96},{16,112},{32,0},{48,16},{64,32},{80,48},{96,64},{112,80},{1... | collective-permute-start | bytes 294920 | tf_op jit(solution)/shard_map/ppermute | solution.py:71
  41.7 10.1 %collective-permute-start.8 = (bf16[64,1024]{0,1:T(8,128)(2,1)S(1)}, bf16[64,1024]{0,1:T(8,128)(2,1)S(1)}, u32[]{:S(2)}, u32[]{:S(2)}) collective-permute-start(bf16[64,1024]{0,1:T(8,128)(2,1)S(1)} %get-tuple-element.199), channel_id=1, source_target_pairs={{0,2},{1,3},{2,0},{3,1},{4,6},{5,7},{6,4},{7,5},{8,10},{9,11},{10,... | collective-permute-start | bytes 393224 | tf_op jit(solution)/shard_map/ppermute | solution.py:63
  52.7 13.1 %collective-permute-start.11 = (bf16[2,64,1024]{1,2,0:T(8,128)(2,1)S(1)}, bf16[2,64,1024]{1,2,0:T(8,128)(2,1)S(1)}, u32[]{:S(2)}, u32[]{:S(2)}) collective-permute-start(bf16[2,64,1024]{1,2,0:T(8,128)(2,1)S(1)} %get-tuple-element.197), channel_id=1, source_target_pairs={{0,8},{1,9},{2,10},{3,11},{4,12},{5,13},{6,14},{7,15},{8,0},{9,1},... | collective-permute-start | bytes 786440 | tf_op jit(solution)/shard_map/ppermute | solution.py:71
  52.7 23.0 %collective-permute-start.10 = (bf16[2,64,1024]{1,2,0:T(8,128)(2,1)S(1)}, bf16[2,64,1024]{1,2,0:T(8,128)(2,1)S(1)}, u32[]{:S(2)}, u32[]{:S(2)}) collective-permute-start(bf16[2,64,1024]{1,2,0:T(8,128)(2,1)S(1)} %get-tuple-element.197), channel_id=1, source_target_pairs={{0,12},{1,13},{2,14},{3,15},{4,0},{5,1},{6,2},{7,3},{8,4},{9,5},{1... | collective-permute-start | bytes 786440 | tf_op jit(solution)/shard_map/ppermute | solution.py:71
  65.9 33.1 %collective-permute-start = (bf16[64,3072]{1,0:T(8,128)(2,1)}, bf16[64,3072]{1,0:T(8,128)(2,1)}, u32[]{:S(2)}, u32[]{:S(2)}) collective-permute-start(bf16[64,3072]{1,0:T(8,128)(2,1)} %get-tuple-element.194), channel_id=1, source_target_pairs={{0,16},{16,0},{32,48},{48,32},{64,80},{80,64},{96,112},{112,96},{1... | collective-permute-start | bytes 1179656 | tf_op jit(solution)/shard_map/ppermute | solution.py:63
  75.8 14.7 %collective-permute-start.9 = (bf16[2,64,1024]{1,2,0:T(8,128)(2,1)S(1)}, bf16[2,64,1024]{1,2,0:T(8,128)(2,1)}, u32[]{:S(2)}, u32[]{:S(2)}) collective-permute-start(bf16[2,64,1024]{1,2,0:T(8,128)(2,1)S(1)} %get-tuple-element.197), channel_id=1, source_target_pairs={{0,4},{1,5},{2,6},{3,7},{4,8},{5,9},{6,10},{7,11},{8,12},{9,13},{1... | collective-permute-start | bytes 786440 | tf_op jit(solution)/shard_map/ppermute | solution.py:71
  96.6 7.6 %collective-permute-start.12 = (bf16[4,2,64,1024]{3,2,1,0:T(8,128)(2,1)}, bf16[4,2,64,1024]{3,2,1,0:T(8,128)(2,1)S(1)}, u32[]{:S(2)}, u32[]{:S(2)}) collective-permute-start(bf16[4,2,64,1024]{3,2,1,0:T(8,128)(2,1)} %copy.70), channel_id=1, source_target_pairs={{0,1},{1,0},{2,3},{3,2},{4,5},{5,4},{6,7},{7,6},{8,9},{9,8},{10,11... | collective-permute-start | bytes 3145736 | tf_op jit(solution)/shard_map/ppermute | solution.py:75
  126.8 11.3 %all-to-all-start = ((bf16[8,128,128]{2,1,0:T(8,128)(2,1)}), bf16[8,128,128]{2,1,0:T(8,128)(2,1)}, u32[]{:S(2)}, u32[]{:S(2)}) async-start(bf16[8,128,128]{2,1,0:T(8,128)(2,1)} %get-tuple-element.77.o_ref.j_ref), calls=%async_computation | async-start | bytes 524288 | tf_op jit(solution)/shard_map/all_to_all | solution.py:715
  131.0 55.4 %all-gather.8.cloned.1.call-start = ((), (), s32[]{:S(2)}) async-start(), calls=%async_computation.5 | async-start | bytes 4456448 | tf_op jit(solution)/shard_map/all_gather | solution.py:716
  147.5 106.5 %all-gather.12.cloned.1.call-start = ((), (), s32[]{:S(2)}) async-start(), calls=%async_computation.8 | async-start | bytes 5013504 | tf_op jit(solution)/shard_map/all_gather | solution.py:702
  151.1 401.9 %all-gather.10.cloned.1.call-start = ((), (), s32[]{:S(2)}) async-start(), calls=%async_computation.7 | async-start | bytes 4456448 | tf_op jit(solution)/shard_map/all_gather | solution.py:718
  188.0 375.2 %reduce-scatter.2.cloned.1.call-start = ((), (), s32[]{:S(2)}) async-start(), calls=%async_computation.6 | async-start | bytes 4456448 | tf_op jit(solution)/shard_map/reduce_scatter | solution.py:737
  188.1 59.7 %collective-permute-start.17 = (bf16[4,64,3072]{2,1,0:T(8,128)(2,1)}, bf16[4,64,3072]{2,1,0:T(8,128)(2,1)}, u32[]{:S(2)}, u32[]{:S(2)}) collective-permute-start(bf16[4,64,3072]{2,1,0:T(8,128)(2,1)} %pad_maximum_fusion.1.refs_5_), channel_id=1, source_target_pairs={{0,16},{16,0},{32,48},{48,32},{64,80},{80,64},{96,112},{112,96},{1... | collective-permute-start | bytes 4718600 | tf_op jit(solution)/shard_map/ppermute | solution.py:63
  190.6 19.9 %collective-permute-start.14 = (bf16[2,64,3072]{2,1,0:T(8,128)(2,1)S(1)}, bf16[2,64,3072]{2,1,0:T(8,128)(2,1)}, u32[]{:S(2)}, u32[]{:S(2)}) collective-permute-start(bf16[2,64,3072]{2,1,0:T(8,128)(2,1)S(1)} %pad_maximum_fusion.2.refs_3_), channel_id=1, source_target_pairs={{0,32},{16,48},{32,64},{48,80},{64,96},{80,112},{96,0},{112,16},{1... | collective-permute-start | bytes 2359304 | tf_op jit(solution)/shard_map/ppermute | solution.py:71
  191.9 18.6 %collective-permute-start.15 = (bf16[2,64,3072]{2,1,0:T(8,128)(2,1)S(1)}, bf16[2,64,3072]{2,1,0:T(8,128)(2,1)}, u32[]{:S(2)}, u32[]{:S(2)}) collective-permute-start(bf16[2,64,3072]{2,1,0:T(8,128)(2,1)S(1)} %pad_maximum_fusion.2.refs_3_), channel_id=1, source_target_pairs={{0,96},{16,112},{32,0},{48,16},{64,32},{80,48},{96,64},{112,80},{1... | collective-permute-start | bytes 2359304 | tf_op jit(solution)/shard_map/ppermute | solution.py:71
  193.3 35.2 %collective-permute-start.16 = (bf16[2,64,3072]{2,1,0:T(8,128)(2,1)S(1)}, bf16[2,64,3072]{2,1,0:T(8,128)(2,1)}, u32[]{:S(2)}, u32[]{:S(2)}) collective-permute-start(bf16[2,64,3072]{2,1,0:T(8,128)(2,1)S(1)} %pad_maximum_fusion.2.refs_3_), channel_id=1, source_target_pairs={{0,64},{16,80},{32,96},{48,112},{64,0},{80,16},{96,32},{112,48},{1... | collective-permute-start | bytes 2359304 | tf_op jit(solution)/shard_map/ppermute | solution.py:71
  290.3 30.2 %collective-permute-start.18 = (bf16[4,2,128,1024]{3,2,1,0:T(8,128)(2,1)}, bf16[4,2,128,1024]{3,2,1,0:T(8,128)(2,1)}, u32[]{:S(2)}, u32[]{:S(2)}) collective-permute-start(bf16[4,2,128,1024]{3,2,1,0:T(8,128)(2,1)} %get-tuple-element.87), channel_id=1, source_target_pairs={{0,1},{1,0},{2,3},{3,2},{4,5},{5,4},{6,7},{7,6},{8,9},{9,8},{10,11... | collective-permute-start | bytes 6291464 | tf_op jit(solution)/shard_map/ppermute | solution.py:75
  322.6 32.0 %collective-permute-start.19 = (bf16[4,64,1024]{2,1,0:T(8,128)(2,1)S(1)}, bf16[4,64,1024]{2,1,0:T(8,128)(2,1)S(1)}, u32[]{:S(2)}, u32[]{:S(2)}) collective-permute-start(bf16[4,64,1024]{2,1,0:T(8,128)(2,1)S(1)} %get-tuple-element.175), channel_id=1, source_target_pairs={{0,2},{1,3},{2,0},{3,1},{4,6},{5,7},{6,4},{7,5},{8,10},{9,11},{10,... | collective-permute-start | bytes 1572872 | tf_op jit(solution)/shard_map/ppermute | solution.py:63
  325.2 29.4 %collective-permute-start.20 = (bf16[2,64,1024]{2,1,0:T(8,128)(2,1)S(1)}, bf16[2,64,1024]{2,1,0:T(8,128)(2,1)S(1)}, u32[]{:S(2)}, u32[]{:S(2)}) collective-permute-start(bf16[2,64,1024]{2,1,0:T(8,128)(2,1)S(1)} %get-tuple-element.174), channel_id=1, source_target_pairs={{0,4},{1,5},{2,6},{3,7},{4,8},{5,9},{6,10},{7,11},{8,12},{9,13},{1... | collective-permute-start | bytes 786440 | tf_op jit(solution)/shard_map/ppermute | solution.py:71
  325.3 29.3 %collective-permute-start.21 = (bf16[2,64,1024]{2,1,0:T(8,128)(2,1)S(1)}, bf16[2,64,1024]{2,1,0:T(8,128)(2,1)S(1)}, u32[]{:S(2)}, u32[]{:S(2)}) collective-permute-start(bf16[2,64,1024]{2,1,0:T(8,128)(2,1)S(1)} %get-tuple-element.173), channel_id=1, source_target_pairs={{0,12},{1,13},{2,14},{3,15},{4,0},{5,1},{6,2},{7,3},{8,4},{9,5},{1... | collective-permute-start | bytes 786440 | tf_op jit(solution)/shard_map/ppermute | solution.py:71
  327.9 26.6 %collective-permute-start.22 = (bf16[2,64,1024]{2,1,0:T(8,128)(2,1)S(1)}, bf16[2,64,1024]{2,1,0:T(8,128)(2,1)S(1)}, u32[]{:S(2)}, u32[]{:S(2)}) collective-permute-start(bf16[2,64,1024]{2,1,0:T(8,128)(2,1)S(1)} %get-tuple-element.172), channel_id=1, source_target_pairs={{0,8},{1,9},{2,10},{3,11},{4,12},{5,13},{6,14},{7,15},{8,0},{9,1},... | collective-permute-start | bytes 786440 | tf_op jit(solution)/shard_map/ppermute | solution.py:71
  352.0 121.3 %collective-permute-start.44 = (bf16[4,64,3072]{2,1,0:T(8,128)(2,1)}, bf16[4,64,3072]{2,1,0:T(8,128)(2,1)}, u32[]{:S(2)}, u32[]{:S(2)}) collective-permute-start(bf16[4,64,3072]{2,1,0:T(8,128)(2,1)} %get-tuple-element.116), channel_id=1, source_target_pairs={{0,16},{16,0},{32,48},{48,32},{64,80},{80,64},{96,112},{112,96},{1... | collective-permute-start | bytes 4718600 | tf_op jit(solution)/shard_map/ppermute | solution.py:63
  354.8 6.2 %collective-permute-start.23 = (bf16[64,1024]{1,0:T(8,128)(2,1)S(1)}, bf16[64,1024]{1,0:T(8,128)(2,1)S(1)}, u32[]{:S(2)}, u32[]{:S(2)}) collective-permute-start(bf16[64,1024]{1,0:T(8,128)(2,1)S(1)} %get-tuple-element.188), channel_id=1, source_target_pairs={{0,4},{1,5},{2,6},{3,7},{4,8},{5,9},{6,10},{7,11},{8,12},{9,13},{1... | collective-permute-start | bytes 393224 | tf_op jit(solution)/shard_map/ppermute | solution.py:71
  357.5 8.1 %collective-permute-start.25 = (bf16[64,1024]{1,0:T(8,128)(2,1)S(1)}, bf16[64,1024]{1,0:T(8,128)(2,1)S(1)}, u32[]{:S(2)}, u32[]{:S(2)}) collective-permute-start(bf16[64,1024]{1,0:T(8,128)(2,1)S(1)} %get-tuple-element.186), channel_id=1, source_target_pairs={{0,8},{1,9},{2,10},{3,11},{4,12},{5,13},{6,14},{7,15},{8,0},{9,1},... | collective-permute-start | bytes 393224 | tf_op jit(solution)/shard_map/ppermute | solution.py:71
  359.4 57.2 %collective-permute-start.26 = (bf16[64,1024]{1,0:T(8,128)(2,1)S(1)}, bf16[64,1024]{1,0:T(8,128)(2,1)S(1)}, u32[]{:S(2)}, u32[]{:S(2)}) collective-permute-start(bf16[64,1024]{1,0:T(8,128)(2,1)S(1)} %get-tuple-element.184), channel_id=1, source_target_pairs={{0,2},{1,3},{2,0},{3,1},{4,6},{5,7},{6,4},{7,5},{8,10},{9,11},{10,... | collective-permute-start | bytes 393224 | tf_op jit(solution)/shard_map/ppermute | solution.py:63
  420.5 10.3 %all-to-all-start.1 = ((bf16[8,128,128]{2,1,0:T(8,128)(2,1)}), bf16[8,128,128]{2,1,0:T(8,128)(2,1)}, u32[]{:S(2)}, u32[]{:S(2)}) async-start(bf16[8,128,128]{2,1,0:T(8,128)(2,1)} %copy-done.42), calls=%async_computation.2 | async-start | bytes 524288 | tf_op jit(solution)/shard_map/all_to_all | solution.py:745
  424.6 48.8 %collective-permute-start.45 = (bf16[2,64,3072]{2,1,0:T(8,128)(2,1)}, bf16[2,64,3072]{2,1,0:T(8,128)(2,1)}, u32[]{:S(2)}, u32[]{:S(2)}) collective-permute-start(bf16[2,64,3072]{2,1,0:T(8,128)(2,1)} %get-tuple-element.117), channel_id=1, source_target_pairs={{0,32},{16,48},{32,64},{48,80},{64,96},{80,112},{96,0},{112,16},{1... | collective-permute-start | bytes 2359304 | tf_op jit(solution)/shard_map/ppermute | solution.py:71
  425.7 47.6 %collective-permute-start.46 = (bf16[2,64,3072]{2,1,0:T(8,128)(2,1)}, bf16[2,64,3072]{2,1,0:T(8,128)(2,1)}, u32[]{:S(2)}, u32[]{:S(2)}) collective-permute-start(bf16[2,64,3072]{2,1,0:T(8,128)(2,1)} %get-tuple-element.118), channel_id=1, source_target_pairs={{0,96},{16,112},{32,0},{48,16},{64,32},{80,48},{96,64},{112,80},{1... | collective-permute-start | bytes 2359304 | tf_op jit(solution)/shard_map/ppermute | solution.py:71
  427.3 46.0 %collective-permute-start.47 = (bf16[2,64,3072]{2,1,0:T(8,128)(2,1)}, bf16[2,64,3072]{2,1,0:T(8,128)(2,1)}, u32[]{:S(2)}, u32[]{:S(2)}) collective-permute-start(bf16[2,64,3072]{2,1,0:T(8,128)(2,1)} %get-tuple-element.119), channel_id=1, source_target_pairs={{0,64},{16,80},{32,96},{48,112},{64,0},{80,16},{96,32},{112,48},{1... | collective-permute-start | bytes 2359304 | tf_op jit(solution)/shard_map/ppermute | solution.py:71
  473.3 8.0 %collective-permute-start.35 = (bf16[128,1024]{1,0:T(8,128)(2,1)S(1)}, bf16[128,1024]{1,0:T(8,128)(2,1)S(1)}, u32[]{:S(2)}, u32[]{:S(2)}) collective-permute-start(bf16[128,1024]{1,0:T(8,128)(2,1)S(1)} %copy-done.44), channel_id=1, source_target_pairs={{0,2},{1,3},{2,0},{3,1},{4,6},{5,7},{6,4},{7,5},{8,10},{9,11},{10,... | collective-permute-start | bytes 786440 | tf_op jit(solution)/shard_map/ppermute | solution.py:63
  477.0 13.8 %collective-permute-start.51 = (bf16[64,3072]{1,0:T(8,128)(2,1)S(1)}, bf16[64,3072]{1,0:T(8,128)(2,1)S(1)}, u32[]{:S(2)}, u32[]{:S(2)}) collective-permute-start(bf16[64,3072]{1,0:T(8,128)(2,1)S(1)} %fusion.8), channel_id=1, source_target_pairs={{0,16},{16,0},{32,48},{48,32},{64,80},{80,64},{96,112},{112,96},{1... | collective-permute-start | bytes 1179656 | tf_op jit(solution)/shard_map/ppermute | solution.py:63
  481.4 12.6 %collective-permute-start.36 = (bf16[2,128,1024]{2,1,0:T(8,128)(2,1)S(1)}, bf16[2,128,1024]{2,1,0:T(8,128)(2,1)S(1)}, u32[]{:S(2)}, u32[]{:S(2)}) collective-permute-start(bf16[2,128,1024]{2,1,0:T(8,128)(2,1)S(1)} %pad_maximum_fusion.5.h3), channel_id=1, source_target_pairs={{0,4},{1,5},{2,6},{3,7},{4,8},{5,9},{6,10},{7,11},{8,12},{9,13},{1... | collective-permute-start | bytes 1572872 | tf_op jit(solution)/shard_map/ppermute | solution.py:71
  483.5 8.6 %collective-permute-start.32 = (f32[17,128]{1,0:T(8,128)S(1)}, f32[17,128]{1,0:T(8,128)S(1)}, u32[]{:S(2)}, u32[]{:S(2)}) collective-permute-start(f32[17,128]{1,0:T(8,128)S(1)} %add.372), channel_id=1, source_target_pairs={{0,16},{16,0},{32,48},{48,32},{64,80},{80,64},{96,112},{112,96},{1... | collective-permute-start | bytes 26120 | tf_op jit(solution)/shard_map/ppermute | solution.py:137
  486.4 27.4 %collective-permute-start.50 = (bf16[64,3072]{1,0:T(8,128)(2,1)S(1)}, bf16[64,3072]{1,0:T(8,128)(2,1)S(1)}, u32[]{:S(2)}, u32[]{:S(2)}) collective-permute-start(bf16[64,3072]{1,0:T(8,128)(2,1)S(1)} %get-tuple-element.178), channel_id=1, source_target_pairs={{0,64},{16,80},{32,96},{48,112},{64,0},{80,16},{96,32},{112,48},{1... | collective-permute-start | bytes 1179656 | tf_op jit(solution)/shard_map/ppermute | solution.py:71
  489.3 24.5 %collective-permute-start.49 = (bf16[64,3072]{1,0:T(8,128)(2,1)S(1)}, bf16[64,3072]{1,0:T(8,128)(2,1)S(1)}, u32[]{:S(2)}, u32[]{:S(2)}) collective-permute-start(bf16[64,3072]{1,0:T(8,128)(2,1)S(1)} %get-tuple-element.179), channel_id=1, source_target_pairs={{0,96},{16,112},{32,0},{48,16},{64,32},{80,48},{96,64},{112,80},{1... | collective-permute-start | bytes 1179656 | tf_op jit(solution)/shard_map/ppermute | solution.py:71
  490.8 23.0 %collective-permute-start.48 = (bf16[64,3072]{1,0:T(8,128)(2,1)S(1)}, bf16[64,3072]{1,0:T(8,128)(2,1)S(1)}, u32[]{:S(2)}, u32[]{:S(2)}) collective-permute-start(bf16[64,3072]{1,0:T(8,128)(2,1)S(1)} %get-tuple-element.177), channel_id=1, source_target_pairs={{0,32},{16,48},{32,64},{48,80},{64,96},{80,112},{96,0},{112,16},{1... | collective-permute-start | bytes 1179656 | tf_op jit(solution)/shard_map/ppermute | solution.py:71
  492.1 9.8 %collective-permute-start.37 = (bf16[2,128,1024]{2,1,0:T(8,128)(2,1)S(1)}, bf16[2,128,1024]{2,1,0:T(8,128)(2,1)S(1)}, u32[]{:S(2)}, u32[]{:S(2)}) collective-permute-start(bf16[2,128,1024]{2,1,0:T(8,128)(2,1)S(1)} %pad_maximum_fusion.5.h3), channel_id=1, source_target_pairs={{0,12},{1,13},{2,14},{3,15},{4,0},{5,1},{6,2},{7,3},{8,4},{9,5},{1... | collective-permute-start | bytes 1572872 | tf_op jit(solution)/shard_map/ppermute | solution.py:71
  494.0 11.8 %collective-permute-start.38 = (bf16[2,128,1024]{2,1,0:T(8,128)(2,1)S(1)}, bf16[2,128,1024]{2,1,0:T(8,128)(2,1)S(1)}, u32[]{:S(2)}, u32[]{:S(2)}) collective-permute-start(bf16[2,128,1024]{2,1,0:T(8,128)(2,1)S(1)} %pad_maximum_fusion.5.h3), channel_id=1, source_target_pairs={{0,8},{1,9},{2,10},{3,11},{4,12},{5,13},{6,14},{7,15},{8,0},{9,1},... | collective-permute-start | bytes 1572872 | tf_op jit(solution)/shard_map/ppermute | solution.py:71
  501.9 13.3 %collective-permute-start.33 = (f32[17,128]{1,0:T(8,128)S(1)}, f32[17,128]{1,0:T(8,128)S(1)}, u32[]{:S(2)}, u32[]{:S(2)}) collective-permute-start(f32[17,128]{1,0:T(8,128)S(1)} %add.373), channel_id=1, source_target_pairs={{0,32},{16,48},{32,0},{48,16},{64,96},{80,112},{96,64},{112,80},{1... | collective-permute-start | bytes 26120 | tf_op jit(solution)/shard_map/ppermute | solution.py:137
  508.2 23.5 %collective-permute-start.39 = (bf16[1024,192]{1,0:T(8,128)(2,1)S(1)}, bf16[1024,192]{1,0:T(8,128)(2,1)}, u32[]{:S(2)}, u32[]{:S(2)}) collective-permute-start(bf16[1024,192]{1,0:T(8,128)(2,1)S(1)} %pad_maximum_fusion.6), channel_id=1, source_target_pairs={{0,1},{1,0},{2,3},{3,2},{4,5},{5,4},{6,7},{7,6},{8,9},{9,8},{10,11... | collective-permute-start | bytes 1179656 | tf_op jit(solution)/shard_map/ppermute | solution.py:75
  515.2 16.5 %collective-permute-start.34 = (f32[17,128]{1,0:T(8,128)S(1)}, f32[17,128]{1,0:T(8,128)S(1)}, u32[]{:S(2)}, u32[]{:S(2)}) collective-permute-start(f32[17,128]{1,0:T(8,128)S(1)} %add.374), channel_id=1, source_target_pairs={{0,64},{16,80},{32,96},{48,112},{64,0},{80,16},{96,32},{112,48},{1... | collective-permute-start | bytes 26120 | tf_op jit(solution)/shard_map/ppermute | solution.py:137
  521.9 37.5 %all-to-all-start.2 = ((bf16[8,128,256]{2,1,0:T(8,128)(2,1)}), bf16[8,128,256]{2,1,0:T(8,128)(2,1)S(1)}, u32[]{:S(2)}, u32[]{:S(2)}) async-start(bf16[8,128,256]{2,1,0:T(8,128)(2,1)} %get-tuple-element.99), calls=%async_computation.3 | async-start | bytes 1048576 | tf_op jit(solution)/shard_map/all_to_all | solution.py:750
  533.2 10.6 %collective-permute-start.40 = (bf16[4,128,192]{1,2,0:T(8,128)(2,1)S(1)}, bf16[4,128,192]{1,2,0:T(8,128)(2,1)S(1)}, u32[]{:S(2)}, u32[]{:S(2)}) collective-permute-start(bf16[4,128,192]{1,2,0:T(8,128)(2,1)S(1)} %bitcast.214), channel_id=1, source_target_pairs={{0,16},{16,0},{32,48},{48,32},{64,80},{80,64},{96,112},{112,96},{1... | collective-permute-start | bytes 589832 | tf_op jit(solution)/shard_map/ppermute | solution.py:63
  (77 other events, 845.5 us)
Sparse Core Ops, SparseCore 0:
  9.7 42.6 all-gather.5
  147.6 38.6 all-gather.7
  188.6 57.0 all-gather.11
  247.2 48.4 all-gather.9
  320.6 86.5 reduce-scatter.1
